TPU v7x, 128 devices: a whole 4x4x4 slice. The times are simulated.
128 devices in a mesh: region: 8 (over y_hi, x), scan: 16 (over y_lo, z, core).
Axes of the slice: x: 4, y: 4 (y_hi: 2, y_lo: 2; y = y_hi * 2 + y_lo), z: 4, core: 2. Of those that a mesh axis runs over, the one named last changes fastest.
Arguments:
- object_real: float32 [2, 4096, 8192], P(None, 'region', 'scan'), may hold values from 0.25 to 1.75
- object_imag: float32 [2, 4096, 8192], P(None, 'region', 'scan'), may hold values from -1.8 to 1.8
- probe_modes: float32 [2, 2, 128, 128], replicated, may hold values from -6 to 6
- amplitudes: float32 [2048, 128, 128], P(('region', 'scan')), may hold values from 0.5 to 4
- offsets: int32 [2048, 2], P(('region', 'scan')), may hold values from 0 to 384
- owners: int32 [2048, 1], P(('region', 'scan')), may hold values from 0 to 15; in each aligned block of 16 rows (0 to 15, 16 to 31, ...) at most 2 rows name the same one
Outputs:
- object_grad: float32 [2, 2, 4096, 8192], P(None, None, 'region', 'scan')
- probe_grad: float32 [2, 2, 128, 128], replicated
Inputs may be any that keep to these rules, and one draw needn't show every extreme that they name: `offsets`: a position's whole patch lies inside the tile that its owner index names. `owners`: each row names a scan index within the region of the device that holds the position; among the 16 rows of one device no index appears more than 2 times, and in every draw some device names some index exactly 2 times.
All inputs are finite; a program needn't handle non-finite values.
Results may differ from a plain program's by a relative error of at most 0.0029.
The roundings to bfloat16 on the way count: a program that leaves them out, or rounds other values in their place, can miss the bound.
Values may be sent and summed in bfloat16 or wider, within the bound.
No kernel may reach another device: no remote copies, remote signals or barrier semaphores. Data moves between devices by JAX's collectives and lax.ppermute only.
A program may use at most 128 MiB of HBM per device.

v0:
```python
import jax
import jax.numpy as jnp
from jax import lax
from jax.sharding import PartitionSpec as P

CAP = 2


fresnel_depth = 20.0
block_rows = 2
highest = lax.Precision.HIGHEST


def fourier_tables(patch_size):
    index = jnp.arange(patch_size, dtype=jnp.int32)
    product = index[:, None] * index[None, :] % patch_size
    angles = 2.0 * jnp.pi / patch_size * product.astype(jnp.float32)
    scale = 1.0 / jnp.sqrt(jnp.float32(patch_size))
    return (jnp.cos(angles) * scale, jnp.sin(angles) * scale)


def make_kernel(patch_size):
    index = jnp.arange(patch_size, dtype=jnp.int32)
    frequency = ((index + patch_size // 2) % patch_size - patch_size // 2).astype(
        jnp.float32
    ) / patch_size
    phase = -jnp.pi * fresnel_depth * (frequency[:, None] ** 2 + frequency[None, :] ** 2)
    return (jnp.cos(phase), jnp.sin(phase))


def right_mul(real_part, imag_part, cosine, signed):
    new_real = jnp.matmul(real_part, cosine, precision=highest) - jnp.matmul(
        imag_part, signed, precision=highest
    )
    new_imag = jnp.matmul(real_part, signed, precision=highest) + jnp.matmul(
        imag_part, cosine, precision=highest
    )
    return (new_real, new_imag)


def left_mul(real_part, imag_part, cosine, signed):
    new_real = jnp.einsum("kn,...nm->...km", cosine, real_part, precision=highest) - jnp.einsum(
        "kn,...nm->...km", signed, imag_part, precision=highest
    )
    new_imag = jnp.einsum("kn,...nm->...km", signed, real_part, precision=highest) + jnp.einsum(
        "kn,...nm->...km", cosine, imag_part, precision=highest
    )
    return (new_real, new_imag)


def transform(real_part, imag_part, tables, inverse):
    cosine, sine = tables
    signed = sine if inverse else -sine
    half_real, half_imag = right_mul(real_part, imag_part, cosine, signed)
    return left_mul(half_real, half_imag, cosine, signed)


def propagate(real_part, imag_part, tables, kernel, adjoint):
    freq_real, freq_imag = transform(real_part, imag_part, tables, False)
    kernel_real, kernel_imag = kernel
    if adjoint:
        kernel_imag = -kernel_imag
    moved_real = freq_real * kernel_real - freq_imag * kernel_imag
    moved_imag = freq_real * kernel_imag + freq_imag * kernel_real
    return transform(moved_real, moved_imag, tables, True)


def position_grads(patch, probe_modes, measured, live_rows, tables, kernel):
    slices = patch.shape[1]
    batch_rows = patch.shape[0]
    trans_real = patch[:, :, 0].astype(jnp.float32)
    trans_imag = patch[:, :, 1].astype(jnp.float32)
    full_shape = (batch_rows,) + probe_modes[:, 0].shape
    wave_real = jnp.broadcast_to(probe_modes[None, :, 0], full_shape)
    wave_imag = jnp.broadcast_to(probe_modes[None, :, 1], full_shape)
    incoming = []
    for layer in range(slices):
        incoming.append((wave_real, wave_imag))
        layer_real = trans_real[:, layer, None]
        layer_imag = trans_imag[:, layer, None]
        wave_real, wave_imag = (
            wave_real * layer_real - wave_imag * layer_imag,
            wave_real * layer_imag + wave_imag * layer_real,
        )
        if layer + 1 < slices:
            wave_real, wave_imag = propagate(wave_real, wave_imag, tables, kernel, False)
    far_real, far_imag = transform(wave_real, wave_imag, tables, False)
    intensity = jnp.sum(far_real * far_real + far_imag * far_imag, axis=1)
    factor = ((1.0 - measured / jnp.sqrt(intensity + 1.0)) * live_rows[:, None, None])[:, None]
    back_real, back_imag = transform(far_real * factor, far_imag * factor, tables, True)
    grads = [None] * slices
    for layer in reversed(range(slices)):
        in_real, in_imag = incoming[layer]
        grad_real = jnp.sum(in_real * back_real + in_imag * back_imag, axis=1)
        grad_imag = jnp.sum(in_real * back_imag - in_imag * back_real, axis=1)
        grads[layer] = jnp.stack([grad_real, grad_imag], axis=1)
        layer_real = trans_real[:, layer, None]
        layer_imag = trans_imag[:, layer, None]
        back_real, back_imag = (
            layer_real * back_real + layer_imag * back_imag,
            layer_real * back_imag - layer_imag * back_real,
        )
        if layer > 0:
            back_real, back_imag = propagate(back_real, back_imag, tables, kernel, True)
    object_terms = jnp.stack(grads, axis=1)
    probe_term = jnp.stack([jnp.sum(back_real, axis=0), jnp.sum(back_imag, axis=0)], axis=1)
    return (object_terms, probe_term)


def cut_patches(tile_stack, corners, patch_size):

    def cut_one(corner):
        anchor = jnp.int32(0)
        row_at = jnp.maximum(corner[0], 0)
        col_at = jnp.maximum(corner[1], 0)
        return lax.dynamic_slice(
            tile_stack,
            (anchor, anchor, row_at, col_at),
            (tile_stack.shape[0], 2, patch_size, patch_size),
        )

    return jax.vmap(cut_one)(corners)


def add_patches(gradient_sum, object_terms, corners):
    slices = object_terms.shape[1]
    patch_size = object_terms.shape[-1]

    def add_one(slot_index, accumulated):
        anchor = jnp.int32(0)
        row_at = jnp.maximum(corners[slot_index, 0], 0)
        col_at = jnp.maximum(corners[slot_index, 1], 0)
        place = (anchor, anchor, row_at, col_at)
        current = lax.dynamic_slice(accumulated, place, (slices, 2, patch_size, patch_size))
        return lax.dynamic_update_slice(accumulated, current + object_terms[slot_index], place)

    return lax.fori_loop(0, object_terms.shape[0], add_one, gradient_sum)


def body(object_real, object_imag, probe_modes, amplitudes, offsets, owners):
    slices = object_real.shape[0]
    tile_side = object_real.shape[1]
    patch_size = probe_modes.shape[-1]
    pos_dev = offsets.shape[0]
    groups = lax.axis_size("scan")
    slot_count = groups * CAP
    tables = fourier_tables(patch_size)
    kernel = make_kernel(patch_size)
    tile_stack = jnp.stack([object_real, object_imag], axis=1).astype(jnp.bfloat16)
    owner_scan = owners[:, 0]
    position_index = jnp.arange(pos_dev, dtype=jnp.int32)
    same_owner = (owner_scan[:, None] == owner_scan[None, :]) & (
        position_index[None, :] < position_index[:, None]
    )
    slot_rank = jnp.sum(same_owner.astype(jnp.int32), axis=1)
    target = owner_scan * CAP + slot_rank
    requests = (
        jnp.full((slot_count, 2), -1, jnp.int32).at[target].set(offsets).reshape(groups, CAP, 2)
    )
    term_shape = (slices, 2, patch_size, patch_size)
    gradient_sum = jnp.zeros((slices, 2, tile_side, tile_side), jnp.float32)
    probe_total = jnp.zeros(probe_modes.shape, jnp.float32)
    arrived = lax.all_to_all(requests, "scan", split_axis=0, concat_axis=0, tiled=True)
    corners = arrived.reshape(slot_count, 2)
    cut_out = cut_patches(tile_stack, corners, patch_size).reshape((groups, CAP) + term_shape)
    fetched = lax.all_to_all(cut_out, "scan", split_axis=0, concat_axis=0, tiled=True).reshape(
        (slot_count,) + term_shape
    )
    own_patches = jnp.take(fetched, target, axis=0)
    all_live = jnp.ones((block_rows,), jnp.float32)

    def block_step(block_index, carry):
        object_terms, probe_acc = carry
        first_row = block_index * block_rows
        patch = lax.dynamic_slice_in_dim(own_patches, first_row, block_rows, 0)
        measured = lax.dynamic_slice_in_dim(amplitudes, first_row, block_rows, 0)
        block_terms, probe_term = position_grads(
            patch, probe_modes, measured, all_live, tables, kernel
        )
        object_terms = lax.dynamic_update_slice_in_dim(
            object_terms, block_terms.astype(jnp.bfloat16), first_row, 0
        )
        return (object_terms, probe_acc + probe_term)

    start_carry = (jnp.zeros((pos_dev,) + term_shape, jnp.bfloat16), probe_total)
    object_terms, probe_total = lax.fori_loop(0, pos_dev // block_rows, block_step, start_carry)
    outgoing = jnp.zeros((slot_count,) + term_shape, jnp.bfloat16).at[target].set(object_terms)
    returned = lax.all_to_all(
        outgoing.reshape((groups, CAP) + term_shape),
        "scan",
        split_axis=0,
        concat_axis=0,
        tiled=True,
    )
    gradient_sum = add_patches(
        gradient_sum, returned.reshape((slot_count,) + term_shape).astype(jnp.float32), corners
    )
    probe_sum = lax.psum(probe_total, ("region", "scan"))
    return (gradient_sum, probe_sum / pos_dev)


def solution(mesh):
    return jax.shard_map(
        body,
        mesh=mesh,
        in_specs=(
            P(None, "region", "scan"),
            P(None, "region", "scan"),
            P(),
            P(("region", "scan"), None, None),
            P(("region", "scan"), None),
            P(("region", "scan"), None),
        ),
        out_specs=(P(None, None, "region", "scan"), P()),
        check_vma=False,
    )
```

profile of v0, /device:TPU:32, one launch (start us, length us, event | category | flops | bytes accessed | tf_op | source)
XLA Modules:
  0.0 954.1 jit_solution(16822867985925796283)
XLA Ops:
  10.9 6.4 all-to-all-start
  17.4 2.5 convert_bitcast_fusion.4
  22.3 3.1 broadcast_in_dim.92.clone
  25.3 83.1 %while.35 = (s32[]{:T(128)}, bf16[2,2,512,512]{3,2,1,0:T(8,128)(2,1)S(1)}, s32[32,4]{0,1:T(4,128)S(1)}, bf16[32,2,2,128,128]{4,3,2,1,0:T(8,128)(2,1)}, s32[]{:T(128)}) while((s32[]{:T(128)}, bf16[2,2,512,512]{3,2,1,0:T(8,128)(2,1)S(1)}, s32[32,4]{0,1:T(4,128)S(1)}, bf16[32,2,2,128,128]{4,3,2,1,0:T(8,128)(2,1)}, s32[]{:T(128)}) %tuple.125), condition=%wide.while_cond, body=%wide.while_body.sunk | while | flops 2 | bytes 263793 | solution.py:116
  25.9 2.0 bitcast_dynamic-update-slice_fusion.2
  108.4 5.9 all-to-all-start.1
  114.5 59.2 %all-to-all-done.1 = bf16[16,2,2,2,128,128]{5,4,3,2,1,0:T(8,128)(2,1)} async-done(((bf16[16,2,2,2,128,128]{5,4,3,2,1,0:T(8,128)(2,1)}), bf16[16,2,2,2,128,128]{5,4,3,2,1,0:T(8,128)(2,1)}, u32[]{:S(2)}, u32[]{:S(2)}) %all-to-all-start.1) | async-done | bytes 4194336 | tf_op jit(solution)/shard_map/all_to_all | solution.py:166
  173.7 3.1 gather_fusion
  180.3 329.6 %while.36 = (s32[]{:T(128)}, bf16[16,2,2,128,128]{4,3,2,1,0:T(8,128)(2,1)}, f32[2,2,128,128]{2,3,0,1:T(8,128)S(1)}, f32[2,2,128,128]{2,3,0,1:T(8,128)S(1)}, bf16...) while((s32[]{:T(128)}, ...), condition=%wide.region_10.11_spmd.clone.clone.clone.clone, body=%wide.region_2.10_spmd.clone.clone.clone.clone.sunk | while | flops 4851974144 | bytes 50005188 | solution.py:186
  509.9 3.1 broadcast_in_dim.92
  513.0 5.1 scatter_fusion
  518.1 7.0 all-to-all-start.2
  526.0 175.7 %all-reduce.2.cloned.1.call-done = f32[2,2,128,128]{3,2,1,0:T(8,128)} async-done(((f32[2,2,128,128]{3,2,1,0:T(8,128)}), f32[2,2,128,128]{3,2,1,0:T(8,128)}) %all-reduce.2.cloned.1.call-update) | async-done | bytes 262160 | tf_op jit(solution)/shard_map/psum | solution.py:198
  703.4 6.5 bitcast_convert_fusion.2
  709.9 2.5 broadcast_in_dim.90
  712.4 234.6 %while.34 = (s32[]{:T(128)}, f32[2,2,512,512]{3,2,1,0:T(8,128)}, s32[32,2]{0,1:T(2,128)S(1)}, f32[32,2,2,128,128]{4,3,2,1,0:T(8,128)}, s32[]{:T(128)}, /*index=5*/s32[1,1]{0,1:T(1,128)}, s32[]{:T(128)}) while((s32[]{:T(128)}, f32[2,2,512,512]{3,2,1,0:T(8,128)}, s32[32,2]{0,1:T(2,128)S(1)}, f32[32,2,2,128,128]{4,3,2,1,0:T(8,128)}, ...), condition=%wide.region_13.14_spmd, body=%wide.region_12.13_spmd.sunk | while | flops 65540 | bytes 1310857 | solution.py:137
  715.5 4.3 dynamic_update_slice.22
  722.8 4.3 dynamic_update_slice.22
  730.2 4.3 dynamic_update_slice.22
  737.5 4.3 dynamic_update_slice.22
  744.9 4.3 dynamic_update_slice.22
  752.3 4.3 dynamic_update_slice.22
  759.6 4.3 dynamic_update_slice.22
  767.0 4.3 dynamic_update_slice.22
  774.3 4.3 dynamic_update_slice.22
  781.7 4.3 dynamic_update_slice.22
  789.0 4.2 dynamic_update_slice.22
  796.2 4.3 dynamic_update_slice.22
  803.6 4.3 dynamic_update_slice.22
  810.9 4.3 dynamic_update_slice.22
  818.3 4.3 dynamic_update_slice.22
  825.6 4.3 dynamic_update_slice.22
  832.9 4.2 dynamic_update_slice.22
  840.2 4.3 dynamic_update_slice.22
  847.6 4.3 dynamic_update_slice.22
  854.9 4.2 dynamic_update_slice.22
  862.2 4.3 dynamic_update_slice.22
  869.5 4.3 dynamic_update_slice.22
  876.9 4.3 dynamic_update_slice.22
  884.2 4.2 dynamic_update_slice.22
  891.5 4.3 dynamic_update_slice.22
  898.9 4.3 dynamic_update_slice.22
  906.2 4.2 dynamic_update_slice.22
  913.5 4.3 dynamic_update_slice.22
  920.8 4.3 dynamic_update_slice.22
  928.2 4.3 dynamic_update_slice.22
  935.5 4.3 dynamic_update_slice.22
  942.9 4.1 dynamic_update_slice.22
  (715 shorter events, 474.4 us)
Async XLA Ops:
  10.9 11.2 %all-to-all-start = ((s32[16,2,2]{1,2,0:T(2,128)}), s32[16,2,2]{1,2,0:T(2,128)S(1)}, u32[]{:S(2)}, u32[]{:S(2)}) async-start(s32[16,2,2]{1,2,0:T(2,128)} %copy.274), calls=%async_computation | async-start | bytes 32768 | tf_op jit(solution)/shard_map/all_to_all | solution.py:163
  108.4 5.9 copy-start.1
  108.4 65.2 %all-to-all-start.1 = ((bf16[16,2,2,2,128,128]{5,4,3,2,1,0:T(8,128)(2,1)}), bf16[16,2,2,2,128,128]{5,4,3,2,1,0:T(8,128)(2,1)}, u32[]{:S(2)}, u32[]{:S(2)}) async-start(bf16[16,2,2,2,128,128]{5,4,3,2,1,0:T(8,128)(2,1)} %bitcast.428), calls=%async_computation.1 | async-start | bytes 8388608 | tf_op jit(solution)/shard_map/all_to_all | solution.py:166
  509.9 3.1 copy-start
  518.1 185.3 %all-to-all-start.2 = ((bf16[16,2,2,2,128,128]{5,4,3,2,1,0:T(8,128)(2,1)}), bf16[16,2,2,2,128,128]{5,4,3,2,1,0:T(8,128)(2,1)}, u32[]{:S(2)}, u32[]{:S(2)}) async-start(bf16[16,2,2,2,128,128]{5,4,3,2,1,0:T(8,128)(2,1)} %bitcast.427), calls=%async_computation.2 | async-start | bytes 8388608 | tf_op jit(solution)/shard_map/all_to_all | solution.py:188
  525.1 176.6 %all-reduce.2.cloned.1.call-start = ((), (), s32[]{:S(2)}) async-start(), calls=%async_computation.3 | async-start | bytes 524288 | tf_op jit(solution)/shard_map/psum | solution.py:198
Sparse Core Ops, SparseCore 0:
  531.3 170.4 all-reduce.1
where the time goes:
time: 962 us; the launch traced here: 954 us
  matrix products  288 us (30%)
  local copies, waits for them, and re-layouts  287 us (30%)
  waiting for transfers between devices  237 us (25%)
  other arithmetic  61.9 us (6%)
  loops' own time  45.9 us (5%)
  starting transfers between devices  19.3 us (2%)
  between operations  14.4 us (1%)
    psum x1, waiting for transfers between devices, body(): probe_sum = lax.psum(probe_total, ('region', 'scan'))  176 us
    dynamic_update_slice x32, local copies, waits for them, and re-layouts, add_one(): lax.dynamic_update_slice(accumulated, current + object_terms[slot_index],...  137 us
    gather x96, local copies, waits for them, and re-layouts  83 us
    all_to_all x1, waiting for transfers between devices, body(): lax.all_to_all(cut_out, 'scan', split_axis=0, concat_axis=0, tiled=True)  59.2 us
    add x32, other arithmetic, add_one(): current + object_terms[slot_index]  41.3 us
    dot_general x48, matrix products, left_mul(): jnp.einsum('kn,...nm->...km', signed, real_part, precision=highest)  39.1 us
    another operation x1, loops' own time, add_patches(): return lax.fori_loop(0, object_terms.shape[0], add_one, gradient_sum)  37.1 us
    dot_general x48, matrix products, right_mul(): jnp.matmul(imag_part, signed, precision=highest)  36.4 us
  transfers between devices with their start and end apart: 4, of which 3 were waited for; matrix products, arithmetic and copies ran while one was open for 1% of the time, Pallas kernels for 0%

commit v1 on v0

v1 whole, which is shorter than its diff:
```python
import functools

import jax
import jax.numpy as jnp
import numpy as np
from jax import lax
from jax.experimental import pallas as pl
from jax.experimental.pallas import tpu as pltpu
from jax.sharding import PartitionSpec as P

BF16 = jnp.bfloat16
F32 = jnp.float32
I32 = jnp.int32

CAP = 2
FRESNEL_DEPTH = 20.0
N = 128
TILE = 512
UNROLL = 4
WIN_ROWS = N + 8
AMP_MID = 2.25
AMP_STEP = 1.75 / 32767.0
VMEM_LIMIT = 56 * 2**20


def operator_tables():
    index = np.arange(N)
    transform = np.exp(-2j * np.pi * (np.outer(index, index) % N) / N) / np.sqrt(N)
    frequency = ((index + N // 2) % N - N // 2) / N
    phase = np.exp(-1j * np.pi * FRESNEL_DEPTH * frequency**2)
    move = np.conj(transform) @ (phase[:, None] * transform)
    tables = []
    for matrix in (move, transform):
        right = np.block([[matrix.real, matrix.imag], [-matrix.imag, matrix.real]])
        for form in (right, right.T):
            form = form.astype(np.float32)
            high = form.astype(BF16)
            low = (form - high.astype(np.float32)).astype(BF16)
            tables += [high, low]
    return tables


def split(value):
    high = value.astype(BF16)
    return high, (value - high.astype(F32)).astype(BF16)


def dot(a, b):
    return jnp.dot(a, b, preferred_element_type=F32)


def right_mul(value, table):
    high, low = split(value)
    return dot(high, table[0]) + dot(low, table[0]) + dot(high, table[1])


def left_mul(value, table):
    high, low = split(value)
    return dot(table[0], high) + dot(table[0], low) + dot(table[1], high)


def blocks(value):
    return [[value[:N, :N], value[:N, N:]], [value[N:, :N], value[N:, N:]]]


def join(parts):
    return jnp.concatenate([jnp.concatenate(row, axis=1) for row in parts], axis=0)


def swap(value):
    (a, b), (c, d) = blocks(value)
    return join([[a, c], [b, d]])


def list_live(index_ref, meta):
    def visit(slot, count):
        source, which = slot // CAP, slot % CAP
        row = index_ref[source, 2 * which]
        col = index_ref[source, 2 * which + 1]
        live = (row >= 0).astype(I32)

        @pl.when(live == 1)
        def _():
            meta[0, count] = slot
            meta[1, count] = row
            meta[2, count] = col
            meta[3, count] = which
            meta[4, count] = 1

        return count + live

    slots = index_ref.shape[0] * CAP
    count = lax.fori_loop(0, slots, visit, jnp.int32(0))
    for extra in range(UNROLL):
        meta[0, count + extra] = 0
        meta[1, count + extra] = 0
        meta[2, count + extra] = 0
        meta[3, count + extra] = 0
        meta[4, count + extra] = 0
    return (count + UNROLL - 1) // UNROLL


def requests_kernel(me_ref, owners_ref, offsets_ref, out_ref, target_ref, seen):
    groups = out_ref.shape[0]
    out_ref[...] = jnp.full(out_ref.shape, -1, I32)
    lane = lax.broadcasted_iota(I32, (1, N), 1)
    for owner in range(groups):
        seen[owner] = 0
    for position in range(owners_ref.shape[0]):
        owner = owners_ref[position, 0]
        rank = seen[owner]
        seen[owner] = rank + 1
        core = (owner ^ me_ref[0] ^ rank) & 1
        device = (owner & ~1) | core
        which = (owner & 1) ^ core
        line = out_ref[pl.ds(device, 1), :]
        line = jnp.where(lane == 2 * which, offsets_ref[position, 0], line)
        line = jnp.where(lane == 2 * which + 1, offsets_ref[position, 1], line)
        out_ref[pl.ds(device, 1), :] = line
        target_ref[position] = device * CAP + which


def amplitudes_kernel(target_ref, amplitudes_ref, out_ref):
    def place(position, carry):
        code = jnp.round((amplitudes_ref[position] - AMP_MID) * (1.0 / AMP_STEP))
        out_ref[target_ref[position]] = code.astype(I32).astype(jnp.int16)
        return carry

    lax.fori_loop(0, amplitudes_ref.shape[0], place, 0)


def forward_kernel(
    index_ref, own_re, own_im, mate_re, mate_im, probe_ref, rah, ral, lah, lal, rwh, rwl, lwh, lwl,
    wave_out, far_out, patch_out,
    meta, window, wave_buf, far_buf, patch_buf, window_sem, out_sem,
):
    n_groups = list_live(index_ref, meta)

    def window_copies(group, half, start):
        for u in range(UNROLL):
            item = group * UNROLL + u
            row = pl.multiple_of(jnp.minimum(meta[1, item] // 8 * 8, TILE - WIN_ROWS), 8)
            col = pl.multiple_of(jnp.minimum(meta[2, item] // N, 2) * N, N)
            for tile, sources in enumerate(((own_re, own_im), (mate_re, mate_im))):
                @pl.when(meta[3, item] == tile)
                def _(sources=sources):
                    for part, source in enumerate(sources):
                        for side in range(2):
                            place = pl.ds(pl.multiple_of(col + side * N, N), N)
                            copy = pltpu.make_async_copy(
                                source.at[:, pl.ds(row, WIN_ROWS), place],
                                window.at[half, u, part, side],
                                window_sem.at[half, u, part, side],
                            )
                            copy.start() if start else copy.wait()

    def out_copies(group, half):
        first = group * UNROLL
        pairs = ((wave_buf, wave_out), (far_buf, far_out), (patch_buf, patch_out))
        return [
            pltpu.make_async_copy(buf.at[half], out.at[pl.ds(first, UNROLL)], out_sem.at[half, i])
            for i, (buf, out) in enumerate(pairs)
        ]

    @pl.when(n_groups > 0)
    def _():
        window_copies(0, 0, True)

    lane = lax.broadcasted_iota(I32, (N, N), 1)

    def step(group, carry):
        half = lax.rem(group, 2)

        @pl.when(group + 1 < n_groups)
        def _():
            window_copies(group + 1, 1 - half, True)

        window_copies(group, half, False)

        @pl.when(group >= 2)
        def _():
            for copy in out_copies(group - 2, half):
                copy.wait()

        waves = []
        for u in range(UNROLL):
            item = group * UNROLL + u
            row, col = meta[1, item], meta[2, item]
            row_in = row - jnp.minimum(row // 8 * 8, TILE - WIN_ROWS)
            shift = col - jnp.minimum(col // N, 2) * N
            back = lax.rem(N - shift, N)
            for layer in range(2):
                for part in range(2):
                    first = window[half, u, part, 0, layer, pl.ds(row_in, N), :]
                    second = window[half, u, part, 1, layer, pl.ds(row_in, N), :]
                    cut = jnp.where(
                        lane < N - shift, pltpu.roll(first, back, 1), pltpu.roll(second, back, 1)
                    )
                    patch_buf[half, u, 2 * layer + part] = cut.astype(BF16)
            p_re = patch_buf[half, u, 0].astype(F32)
            p_im = patch_buf[half, u, 1].astype(F32)
            rows = []
            for mode in range(2):
                w_re, w_im = probe_ref[mode, 0], probe_ref[mode, 1]
                rows.append([w_re * p_re - w_im * p_im, w_re * p_im + w_im * p_re])
            waves.append(join(rows))
        waves = [right_mul(w, (rah[...], ral[...])) for w in waves]
        waves = [left_mul(swap(w), (lah[...], lal[...])) for w in waves]
        for u in range(UNROLL):
            wave_buf[half, u] = waves[u]
            p_re = patch_buf[half, u, 2].astype(F32)
            p_im = patch_buf[half, u, 3].astype(F32)
            w = blocks(waves[u])
            waves[u] = join(
                [
                    [w[0][m] * p_re - w[1][m] * p_im, w[0][m] * p_im + w[1][m] * p_re]
                    for m in range(2)
                ]
            )
        waves = [right_mul(w, (rwh[...], rwl[...])) for w in waves]
        waves = [left_mul(swap(w), (lwh[...], lwl[...])) for w in waves]
        for u in range(UNROLL):
            far_buf[half, u] = waves[u]
        for copy in out_copies(group, half):
            copy.start()
        return carry

    lax.fori_loop(0, n_groups, step, 0)
    for before in (2, 1):

        @pl.when(n_groups >= before)
        def _(before=before):
            for copy in out_copies(n_groups - before, lax.rem(n_groups - before, 2)):
                copy.wait()


def backward_kernel(
    index_ref, codes_ref, wave_in, far_in, patch_in, probe_ref, rah, ral, lah, lal, rwh, rwl, lwh, lwl,
    own_out, mate_out, probe_out,
    meta, total, wave_buf, far_buf, patch_buf, in_sem, out_sem,
):
    n_groups = list_live(index_ref, meta)

    def in_copies(group, half):
        first = group * UNROLL
        pairs = ((wave_in, wave_buf), (far_in, far_buf), (patch_in, patch_buf))
        return [
            pltpu.make_async_copy(src.at[pl.ds(first, UNROLL)], buf.at[half], in_sem.at[half, i])
            for i, (src, buf) in enumerate(pairs)
        ]

    @pl.when(n_groups > 0)
    def _():
        for copy in in_copies(0, 0):
            copy.start()

    total[...] = jnp.zeros(total.shape, F32)
    probe_out[...] = jnp.zeros(probe_out.shape, F32)
    lane = lax.broadcasted_iota(I32, (N, N), 1)

    def add_patch(item, plane, value):
        row, col, tile = meta[1, item], meta[2, item], meta[3, item]
        first = jnp.minimum(col // N, 2)
        shift = col - first * N
        moved = pltpu.roll(value.astype(BF16).astype(F32), lax.rem(shift, N), 1)
        here = (tile, plane, first, pl.ds(row, N))
        there = (tile, plane, first + 1, pl.ds(row, N))
        total[here] = total[here] + jnp.where(lane >= shift, moved, 0.0)
        total[there] = total[there] + jnp.where(lane < shift, moved, 0.0)

    def step(group, carry):
        half = lax.rem(group, 2)

        @pl.when(group + 1 < n_groups)
        def _():
            for copy in in_copies(group + 1, 1 - half):
                copy.start()

        for copy in in_copies(group, half):
            copy.wait()

        waves = []
        for u in range(UNROLL):
            item = group * UNROLL + u
            far = blocks(far_buf[half, u])
            intensity = sum(far[c][m] * far[c][m] for c in range(2) for m in range(2))
            code = codes_ref[meta[0, item]].astype(I32).astype(F32)
            measured = code * AMP_STEP + AMP_MID
            factor = (1.0 - measured * lax.rsqrt(intensity + 1.0)) * meta[4, item].astype(F32)
            waves.append(join([[far[c][m] * factor for m in range(2)] for c in range(2)]))
        waves = [left_mul(w, (rwh[...], rwl[...])) for w in waves]
        waves = [right_mul(swap(w), (lwh[...], lwl[...])) for w in waves]
        for u in range(UNROLL):
            item = group * UNROLL + u
            back = blocks(waves[u])
            wave = blocks(wave_buf[half, u])
            add_patch(
                item, 2, sum(wave[0][m] * back[m][0] + wave[1][m] * back[m][1] for m in range(2))
            )
            add_patch(
                item, 3, sum(wave[0][m] * back[m][1] - wave[1][m] * back[m][0] for m in range(2))
            )
            p_re = patch_buf[half, u, 2].astype(F32)
            p_im = patch_buf[half, u, 3].astype(F32)
            waves[u] = join(
                [
                    [
                        p_re * back[m][0] + p_im * back[m][1],
                        p_re * back[m][1] - p_im * back[m][0],
                    ]
                    for m in range(2)
                ]
            )
        waves = [right_mul(w, (lah[...], lal[...])) for w in waves]
        waves = [left_mul(swap(w), (rah[...], ral[...])) for w in waves]
        terms = [[0.0, 0.0], [0.0, 0.0]]
        for u in range(UNROLL):
            item = group * UNROLL + u
            back = blocks(waves[u])
            probe = [[probe_ref[m, c] for c in range(2)] for m in range(2)]
            add_patch(
                item, 0, sum(probe[m][0] * back[0][m] + probe[m][1] * back[1][m] for m in range(2))
            )
            add_patch(
                item, 1, sum(probe[m][0] * back[1][m] - probe[m][1] * back[0][m] for m in range(2))
            )
            p_re = patch_buf[half, u, 0].astype(F32)
            p_im = patch_buf[half, u, 1].astype(F32)
            for m in range(2):
                terms[m][0] = terms[m][0] + (p_re * back[0][m] + p_im * back[1][m])
                terms[m][1] = terms[m][1] + (p_re * back[1][m] - p_im * back[0][m])
        for m in range(2):
            for c in range(2):
                probe_out[m, c] += terms[m][c]
        return carry

    lax.fori_loop(0, n_groups, step, 0)
    copies = [
        pltpu.make_async_copy(
            total.at[tile, pl.ds(2 * layer, 2), side],
            out.at[layer, :, :, pl.ds(side * N, N)],
            out_sem.at[tile, layer, side],
        )
        for tile, out in enumerate((own_out, mate_out))
        for layer in range(2)
        for side in range(TILE // N)
    ]
    for copy in copies:
        copy.start()
    for copy in copies:
        copy.wait()


def spec(space):
    return pl.BlockSpec(memory_space=space)


def reduce_probe(part):
    axes = ("region", "scan")
    devices = lax.axis_size("region") * lax.axis_size("scan")
    chips = devices // 2
    mates = [(i, i ^ 1) for i in range(devices)]
    same_core = [list(range(core, devices, 2)) for core in range(2)]
    core = lax.axis_index("scan") & 1
    halves = part.reshape(2, chips, -1)
    kept = lax.dynamic_index_in_dim(halves, core, 0, False)
    given = lax.dynamic_index_in_dim(halves, 1 - core, 0, False)
    mine = kept + lax.ppermute(given, axes, mates)
    pieces = lax.all_to_all(mine, axes, 0, 0, axis_index_groups=same_core, tiled=True)
    piece = jnp.sum(pieces, axis=0, keepdims=True)
    half = lax.all_to_all(
        jnp.broadcast_to(piece, pieces.shape), axes, 0, 0, axis_index_groups=same_core, tiled=True
    )
    other = lax.ppermute(half, axes, mates)
    whole = jnp.where(core == 0, jnp.stack([half, other]), jnp.stack([other, half]))
    return whole.reshape(part.shape)


def body(object_real, object_imag, probe_modes, amplitudes, offsets, owners):
    groups = lax.axis_size("scan")
    pos_dev = offsets.shape[0]
    slots = groups * CAP
    vmem, smem, anywhere = spec(pltpu.VMEM), spec(pltpu.SMEM), spec(pl.ANY)
    params = pltpu.CompilerParams(vmem_limit_bytes=VMEM_LIMIT)
    mates = [(i, i ^ 1) for i in range(groups)]
    tables = [jnp.asarray(t) for t in operator_tables()]
    me = lax.axis_index("scan").astype(I32).reshape(1)

    requests, target = pl.pallas_call(
        requests_kernel,
        out_shape=(
            jax.ShapeDtypeStruct((groups, N), I32),
            jax.ShapeDtypeStruct((pos_dev,), I32),
        ),
        in_specs=[smem, smem, smem],
        out_specs=(vmem, smem),
        scratch_shapes=[pltpu.SMEM((groups,), I32)],
        name="requests",
    )(me, owners, offsets)
    arrived = lax.all_to_all(requests, "scan", 0, 0, tiled=True)
    mate_real = lax.ppermute(object_real, "scan", mates)
    mate_imag = lax.ppermute(object_imag, "scan", mates)
    codes = pl.pallas_call(
        amplitudes_kernel,
        out_shape=jax.ShapeDtypeStruct((slots, N, N), jnp.int16),
        in_specs=[smem, vmem],
        out_specs=vmem,
        compiler_params=params,
        name="amplitudes",
    )(target, amplitudes)
    codes = lax.all_to_all(
        codes.reshape(groups, CAP, N, N), "scan", 0, 0, tiled=True
    ).reshape(slots, N, N)

    two = 2 * N
    flops = slots * 4 * 3 * 2 * two**3
    waves, fars, patches = pl.pallas_call(
        forward_kernel,
        out_shape=(
            jax.ShapeDtypeStruct((slots, two, two), F32),
            jax.ShapeDtypeStruct((slots, two, two), F32),
            jax.ShapeDtypeStruct((slots, 4, N, N), BF16),
        ),
        in_specs=[smem] + [anywhere] * 4 + [vmem] * 9,
        out_specs=(anywhere,) * 3,
        scratch_shapes=[
            pltpu.SMEM((5, slots + UNROLL), I32),
            pltpu.VMEM((2, UNROLL, 2, 2, 2, WIN_ROWS, N), F32),
            pltpu.VMEM((2, UNROLL, two, two), F32),
            pltpu.VMEM((2, UNROLL, two, two), F32),
            pltpu.VMEM((2, UNROLL, 4, N, N), BF16),
            pltpu.SemaphoreType.DMA((2, UNROLL, 2, 2)),
            pltpu.SemaphoreType.DMA((2, 3)),
        ],
        compiler_params=params,
        cost_estimate=pl.CostEstimate(flops=flops, bytes_accessed=40 * 2**20, transcendentals=0),
        name="forward",
    )(arrived, object_real, object_imag, mate_real, mate_imag, probe_modes, *tables)
    grad_shape = jax.ShapeDtypeStruct((2, 2, TILE, TILE), F32)
    own_grad, mate_grad, probe_part = pl.pallas_call(
        backward_kernel,
        out_shape=(grad_shape, grad_shape, jax.ShapeDtypeStruct((2, 2, N, N), F32)),
        in_specs=[smem, vmem] + [anywhere] * 3 + [vmem] * 9,
        out_specs=(anywhere, anywhere, vmem),
        scratch_shapes=[
            pltpu.SMEM((5, slots + UNROLL), I32),
            pltpu.VMEM((2, 4, TILE // N, TILE, N), F32),
            pltpu.VMEM((2, UNROLL, two, two), F32),
            pltpu.VMEM((2, UNROLL, two, two), F32),
            pltpu.VMEM((2, UNROLL, 4, N, N), BF16),
            pltpu.SemaphoreType.DMA((2, 3)),
            pltpu.SemaphoreType.DMA((2, 2, TILE // N)),
        ],
        compiler_params=params,
        cost_estimate=pl.CostEstimate(flops=flops, bytes_accessed=40 * 2**20, transcendentals=0),
        name="backward",
    )(arrived, codes, waves, fars, patches, probe_modes, *tables)
    object_grad = own_grad + lax.ppermute(mate_grad, "scan", mates)
    return object_grad, reduce_probe(probe_part) / pos_dev


def solution(mesh):
    return jax.shard_map(
        body,
        mesh=mesh,
        in_specs=(
            P(None, "region", "scan"),
            P(None, "region", "scan"),
            P(),
            P(("region", "scan"), None, None),
            P(("region", "scan"), None),
            P(("region", "scan"), None),
        ),
        out_specs=(P(None, None, "region", "scan"), P()),
        check_vma=False,
    )
```

time: 962 us -> 117 us (0.12)
  the two profiles are of different devices: /device:TPU:32 before, /device:TPU:1 now
where the time goes in v1:
time: 117 us; the launch traced here: 115 us
  Pallas kernels  45.6 us (39%)
  blocking collectives  29.7 us (25%)
  starting transfers between devices  16 us (14%)
  waiting for transfers between devices  9.79 us (8%)
  other arithmetic  7.35 us (6%)
  local copies, waits for them, and re-layouts  6.22 us (5%)
    pallas_call x1, Pallas kernels, body(): pl.pallas_call(backward_kernel, out_shape=(grad_shape, grad_shape, jax.Sh...  22.7 us
    pallas_call x1, Pallas kernels, body(): pl.pallas_call(forward_kernel, out_shape=(jax.ShapeDtypeStruct((slots, tw...  18.8 us
    all_to_all x1, blocking collectives, reduce_probe(): lax.all_to_all(mine, axes, 0, 0, axis_index_groups=same_core, tiled=True)  16.2 us
    all_to_all x1, blocking collectives, reduce_probe(): lax.all_to_all(jnp.broadcast_to(piece, pieces.shape), axes, 0, 0, axis_in...  13.4 us
    all_to_all x1, starting transfers between devices, body(): arrived = lax.all_to_all(requests, 'scan', 0, 0, tiled=True)  6.85 us
    add x1, other arithmetic, body(): object_grad = own_grad + lax.ppermute(mate_grad, 'scan', mates)  6.49 us
    ppermute x1, waiting for transfers between devices, reduce_probe(): mine = kept + lax.ppermute(given, axes, mates)  5.73 us
    unnamed x9, local copies, waits for them, and re-layouts  5.03 us
  transfers between devices with their start and end apart: 7, of which 3 were waited for; matrix products, arithmetic and copies ran while one was open for 4% of the time, Pallas kernels for 20%

profile of v1, /device:TPU:1, one launch (start us, length us, event | category | flops | bytes accessed | tf_op | source)
XLA Modules:
  0.0 115.3 jit_solution(1758578943710016307)
XLA Ops:
  0.6 1.5 %collective-permute-start = (f32[2,512,512]{2,1,0:T(8,128)}, f32[2,512,512]{2,1,0:T(8,128)S(1)}, u32[]{:S(2)}, u32[]{:S(2)}) collective-permute-start(f32[2,512,512]{2,1,0:T(8,128)} %own_re.1), channel_id=1, source_target_pairs={{0,1},{1,0},{2,3},{3,2},{4,5},{5,4},{6,7},{7,6},{8,9},{9,8},{10,11... | collective-permute-start | bytes 6291464 | tf_op jit(solution)/shard_map/ppermute | solution.py:401
  2.1 0.1 collective-permute-start.1
  2.2 1.3 %copy.18.owners_ref = s32[16,1]{1,0:T(8,128)} copy(s32[16,1]{0,1:T(1,128)} %param.19) | data formatting | bytes 128 | tf_op args[5]
  3.6 1.4 %copy.19.offsets_ref = s32[16,2]{1,0:T(8,128)} copy(s32[16,2]{0,1:T(2,128)} %param.18) | data formatting | bytes 256 | tf_op args[4]
  4.9 1.6 %requests.1 = (s32[16,128]{1,0:T(8,128)}, s32[16]{0:T(128)}) custom-call(s32[1]{0:T(128)} %bitcast.me_ref, s32[16,1]{1,0:T(8,128)} %copy.18.owners_ref, s32[16,2]{1,0:T(8,128)} %copy.19.offsets_ref), custom_call_target="tpu_custom_call" | custom-call | tf_op jit(solution)/shard_map/requests/pallas_call | solution.py:389
  6.5 6.8 %all-to-all-start = ((s32[16,1,128]{2,1,0:T(1,128)}), s32[16,1,128]{2,1,0:T(1,128)S(1)}, u32[]{:S(2)}, u32[]{:S(2)}) async-start(s32[16,1,128]{2,1,0:T(1,128)} %bitcast.23), calls=%async_computation | async-start | bytes 16384 | tf_op jit(solution)/shard_map/all_to_all | solution.py:400
  13.4 2.4 %amplitudes.1 = s16[32,128,128]{2,1,0:T(8,128)(2,1)} custom-call(s32[16]{0:T(128)} %get-tuple-element.11.target_ref, f32[16,128,128]{2,1,0:T(8,128)} %amplitudes_ref.1), custom_call_target="tpu_custom_call" | custom-call | tf_op jit(solution)/shard_map/amplitudes/pallas_call | solution.py:403
  15.8 3.1 %all-to-all-done = s32[16,1,128]{2,1,0:T(1,128)S(1)} async-done(((s32[16,1,128]{2,1,0:T(1,128)}), s32[16,1,128]{2,1,0:T(1,128)S(1)}, u32[]{:S(2)}, u32[]{:S(2)}) %all-to-all-start) | async-done | bytes 8224 | tf_op jit(solution)/shard_map/all_to_all | solution.py:400
  18.9 0.0 copy-start.1
  18.9 4.0 %all-to-all-start.1 = ((s16[16,2,128,128]{3,2,1,0:T(8,128)(2,1)}), s16[16,2,128,128]{3,2,1,0:T(8,128)(2,1)S(1)}, u32[]{:S(2)}, u32[]{:S(2)}) async-start(s16[16,2,128,128]{3,2,1,0:T(8,128)(2,1)} %bitcast.17), calls=%async_computation.1 | async-start | bytes 2097152 | tf_op jit(solution)/shard_map/all_to_all | solution.py:411
  22.8 0.0 collective-permute-done.mate_re
  22.8 0.0 copy-start.2
  22.9 0.0 collective-permute-done.1.mate_im
  22.9 0.0 copy-done.1
  22.9 1.3 %copy-done.2 = f32[2,512,512]{2,1,0:T(8,128)} copy-done((f32[2,512,512]{2,1,0:T(8,128)}, f32[2,512,512]{2,1,0:T(8,128)S(1)}, u32[]{:S(2)}) %copy-start.2) | copy-done | bytes 2097176
  24.2 18.8 %forward.1 = (f32[32,256,256]{2,1,0:T(8,128)}, f32[32,256,256]{2,1,0:T(8,128)}, bf16[32,4,128,128]{3,2,1,0:T(8,128)(2,1)}) custom-call(s32[16,128]{1,0:T(8,128)} %bitcast.21, f32[2,512,512]{2,1,0:T(8,128)} %own_re.1, f32[2,512,512]{2,1,0:T(8,128)} %own_im.1, f32[2,512,512]{2,1,0:T(8,128)} %copy-done.2, f32[2,512,512]{2,1,0:T(8,128)} %collective-permute-done.1.mate_im, ...), custom_call_target="tpu_custom_call" | custom-call | flops 12884901888 | bytes 41943040 | tf_op jit(solution)/shard_map/forward/pallas_call | solution.py:417
  43.0 0.0 all-to-all-done.1
  43.0 0.0 copy-start
  43.0 1.0 copy-done
  44.1 22.7 %backward.1 = (f32[2,2,512,512]{3,2,1,0:T(8,128)}, f32[2,2,512,512]{3,2,1,0:T(8,128)}, f32[2,2,128,128]{3,2,1,0:T(8,128)}) custom-call(s32[16,128]{1,0:T(8,128)} %bitcast.22, s16[32,128,128]{2,1,0:T(8,128)(2,1)} %bitcast.19, f32[32,256,256]{2,1,0:T(8,128)} %get-tuple-element.12.wave_in, f32[32,256,256]{2,1,0:T(8,128)} %get-tuple-element.13.far_in, ...), custom_call_target="tpu_custom_call" | custom-call | flops 12884901888 | bytes 41943040 | tf_op jit(solution)/shard_map/backward/pallas_call | solution.py:440
  66.8 0.4 collective-permute-start.2
  67.2 1.0 reshape.39
  68.2 0.3 collective-permute-start.3
  68.5 5.7 %collective-permute-done.3 = f32[64,512]{1,0:T(8,128)S(1)} collective-permute-done((f32[64,512]{1,0:T(8,128)S(1)}, f32[64,512]{1,0:T(8,128)S(1)}, u32[]{:S(2)}, u32[]{:S(2)}) %collective-permute-start.3) | collective-permute-done | bytes 131104 | tf_op jit(solution)/shard_map/ppermute | solution.py:368
  74.2 0.1 all_to_all.26
  74.3 16.2 %all_to_all.34 = f32[64,1,512]{2,1,0:T(1,128)S(1)} all-to-all(f32[64,1,512]{2,1,0:T(1,128)S(1)} %all_to_all.26), channel_id=1, replica_groups={{0,2,4,6,8,10,12,14,16,18,20,22,24,26,28,30,32,34,36,38,40,42,44,46,48,..., dimensions={0} | all-to-all | bytes 262144 | tf_op jit(solution)/shard_map/all_to_all | solution.py:369
  90.6 0.1 reduce_sum.9
  90.7 0.1 broadcast_in_dim.2
  90.8 13.4 %all_to_all.35 = f32[64,1,512]{2,1,0:T(1,128)S(1)} all-to-all(f32[64,1,512]{2,1,0:T(1,128)S(1)} %broadcast_in_dim.2), channel_id=1, replica_groups={{0,2,4,6,8,10,12,14,16,18,20,22,24,26,28,30,32,34,36,38,40,42,44,46,48,..., dimensions={0} | all-to-all | bytes 262144 | tf_op jit(solution)/shard_map/all_to_all | solution.py:371
  104.2 2.9 %collective-permute-start.4 = (f32[64,512]{1,0:T(8,128)S(1)}, f32[64,512]{1,0:T(8,128)S(1)}, u32[]{:S(2)}, u32[]{:S(2)}) collective-permute-start(f32[64,512]{1,0:T(8,128)S(1)} %bitcast.20), channel_id=1, source_target_pairs={{0,1},{1,0},{2,3},{3,2},{4,5},{5,4},{6,7},{7,6},{8,9},{9,8},{10,11... | collective-permute-start | bytes 393224 | tf_op jit(solution)/shard_map/ppermute | solution.py:374
  107.1 1.0 collective-permute-done.4
  108.1 0.7 fusion
  108.8 0.0 collective-permute-done.2
  108.8 6.5 %add.14 = f32[2,2,512,512]{3,2,1,0:T(8,128)} add(f32[2,2,512,512]{3,2,1,0:T(8,128)} %get-tuple-element.15, f32[2,2,512,512]{3,2,1,0:T(8,128)} %collective-permute-done.2) | non-fusion elementwise | flops 1048576 | bytes 12582912 | tf_op jit(solution)/shard_map/add | solution.py:458
  (4 shorter events, 0.1 us)
Async XLA Ops:
  0.6 22.2 %collective-permute-start = (f32[2,512,512]{2,1,0:T(8,128)}, f32[2,512,512]{2,1,0:T(8,128)S(1)}, u32[]{:S(2)}, u32[]{:S(2)}) collective-permute-start(f32[2,512,512]{2,1,0:T(8,128)} %own_re.1), channel_id=1, source_target_pairs={{0,1},{1,0},{2,3},{3,2},{4,5},{5,4},{6,7},{7,6},{8,9},{9,8},{10,11... | collective-permute-start | bytes 6291464 | tf_op jit(solution)/shard_map/ppermute | solution.py:401
  2.1 20.7 %collective-permute-start.1 = (f32[2,512,512]{2,1,0:T(8,128)}, f32[2,512,512]{2,1,0:T(8,128)}, u32[]{:S(2)}, u32[]{:S(2)}) collective-permute-start(f32[2,512,512]{2,1,0:T(8,128)} %own_im.1), channel_id=1, source_target_pairs={{0,1},{1,0},{2,3},{3,2},{4,5},{5,4},{6,7},{7,6},{8,9},{9,8},{10,11... | collective-permute-start | bytes 6291464 | tf_op jit(solution)/shard_map/ppermute | solution.py:402
  6.5 12.3 %all-to-all-start = ((s32[16,1,128]{2,1,0:T(1,128)}), s32[16,1,128]{2,1,0:T(1,128)S(1)}, u32[]{:S(2)}, u32[]{:S(2)}) async-start(s32[16,1,128]{2,1,0:T(1,128)} %bitcast.23), calls=%async_computation | async-start | bytes 16384 | tf_op jit(solution)/shard_map/all_to_all | solution.py:400
  18.9 4.0 %copy-start.1 = (s32[16,1,128]{2,1,0:T(1,128)}, s32[16,1,128]{2,1,0:T(1,128)S(1)}, u32[]{:S(2)}) copy-start(s32[16,1,128]{2,1,0:T(1,128)S(1)} %all-to-all-done) | copy-start | bytes 24580
  18.9 24.1 %all-to-all-start.1 = ((s16[16,2,128,128]{3,2,1,0:T(8,128)(2,1)}), s16[16,2,128,128]{3,2,1,0:T(8,128)(2,1)S(1)}, u32[]{:S(2)}, u32[]{:S(2)}) async-start(s16[16,2,128,128]{3,2,1,0:T(8,128)(2,1)} %bitcast.17), calls=%async_computation.1 | async-start | bytes 2097152 | tf_op jit(solution)/shard_map/all_to_all | solution.py:411
  22.8 1.3 %copy-start.2 = (f32[2,512,512]{2,1,0:T(8,128)}, f32[2,512,512]{2,1,0:T(8,128)S(1)}, u32[]{:S(2)}) copy-start(f32[2,512,512]{2,1,0:T(8,128)S(1)} %collective-permute-done.mate_re) | copy-start | bytes 6291460
  43.0 1.1 copy-start
  66.8 42.0 %collective-permute-start.2 = (f32[2,2,512,512]{3,2,1,0:T(8,128)}, f32[2,2,512,512]{3,2,1,0:T(8,128)}, u32[]{:S(2)}, u32[]{:S(2)}) collective-permute-start(f32[2,2,512,512]{3,2,1,0:T(8,128)} %get-tuple-element.16), channel_id=1, source_target_pairs={{0,1},{1,0},{2,3},{3,2},{4,5},{5,4},{6,7},{7,6},{8,9},{9,8},{10,11... | collective-permute-start | bytes 12582920 | tf_op jit(solution)/shard_map/ppermute | solution.py:458
  68.2 6.0 %collective-permute-start.3 = (f32[64,512]{1,0:T(8,128)S(1)}, f32[64,512]{1,0:T(8,128)S(1)}, u32[]{:S(2)}, u32[]{:S(2)}) collective-permute-start(f32[64,512]{1,0:T(8,128)S(1)} %dynamic-slice_bitcast_fusion), channel_id=1, source_target_pairs={{0,1},{1,0},{2,3},{3,2},{4,5},{5,4},{6,7},{7,6},{8,9},{9,8},{10,11... | collective-permute-start | bytes 393224 | tf_op jit(solution)/shard_map/ppermute | solution.py:368
  104.2 3.9 %collective-permute-start.4 = (f32[64,512]{1,0:T(8,128)S(1)}, f32[64,512]{1,0:T(8,128)S(1)}, u32[]{:S(2)}, u32[]{:S(2)}) collective-permute-start(f32[64,512]{1,0:T(8,128)S(1)} %bitcast.20), channel_id=1, source_target_pairs={{0,1},{1,0},{2,3},{3,2},{4,5},{5,4},{6,7},{7,6},{8,9},{9,8},{10,11... | collective-permute-start | bytes 393224 | tf_op jit(solution)/shard_map/ppermute | solution.py:374

commit v2 on v0

v2 whole, which is shorter than its diff:
```python
import functools

import jax
import jax.numpy as jnp
import numpy as np
from jax import lax
from jax.experimental import pallas as pl
from jax.experimental.pallas import tpu as pltpu
from jax.sharding import PartitionSpec as P

BF16 = jnp.bfloat16
F32 = jnp.float32
I32 = jnp.int32

CAP = 2
FRESNEL_DEPTH = 20.0
N = 128
TILE = 512
UNROLL = 4
WIN_ROWS = N + 8
TAIL = 16
AMP_MID = 2.25
AMP_STEP = 1.75 / 32767.0
VMEM_LIMIT = 56 * 2**20


def operator_tables():
    index = np.arange(N)
    transform = np.exp(-2j * np.pi * (np.outer(index, index) % N) / N) / np.sqrt(N)
    frequency = ((index + N // 2) % N - N // 2) / N
    phase = np.exp(-1j * np.pi * FRESNEL_DEPTH * frequency**2)
    move = np.conj(transform) @ (phase[:, None] * transform)
    tables = []
    for matrix in (move, transform):
        right = np.block([[matrix.real, matrix.imag], [-matrix.imag, matrix.real]])
        for form in (right, right.T):
            form = form.astype(np.float32)
            high = form.astype(BF16)
            low = (form - high.astype(np.float32)).astype(BF16)
            tables += [high, low]
    return tables


def split(value):
    high = value.astype(BF16)
    return high, (value - high.astype(F32)).astype(BF16)


def dot(a, b):
    return jnp.dot(a, b, preferred_element_type=F32)


def right_mul(value, table):
    high, low = split(value)
    return dot(high, table[0]) + dot(low, table[0]) + dot(high, table[1])


def left_mul(value, table):
    high, low = split(value)
    return dot(table[0], high) + dot(table[0], low) + dot(table[1], high)


def blocks(value):
    return [[value[:N, :N], value[:N, N:]], [value[N:, :N], value[N:, N:]]]


def join(parts):
    return jnp.concatenate([jnp.concatenate(row, axis=1) for row in parts], axis=0)


def list_live(corner_ref, meta):
    slots = corner_ref.shape[0] // 2

    def visit(which):
        def look(source, count):
            slot = source * CAP + which
            row = corner_ref[2 * slot]
            live = (row >= 0).astype(I32)

            @pl.when(live == 1)
            def _():
                meta[0, count] = slot
                meta[1, count] = row
                meta[2, count] = corner_ref[2 * slot + 1]
                meta[3, count] = which
                meta[4, count] = 1

            return count + live

        return look

    n_mate = lax.fori_loop(0, slots // CAP, visit(1), jnp.int32(0))
    count = lax.fori_loop(0, slots // CAP, visit(0), n_mate)
    for extra in range(UNROLL):
        for field in range(5):
            meta[field, count + extra] = 0
    return n_mate, count


def prepare_kernel(me_ref, owners_ref, offsets_ref, amplitudes_ref, out_ref, seen):
    for owner in range(out_ref.shape[0] // CAP):
        seen[owner] = 0
    out_ref[:, N:, :] = jnp.full((out_ref.shape[0], TAIL, N), -1, jnp.int16)
    lane = lax.broadcasted_iota(I32, (TAIL, N), 1)

    def place(position, carry):
        owner = owners_ref[position]
        rank = seen[owner]
        seen[owner] = rank + 1
        core = (owner ^ me_ref[0] ^ rank) & 1
        slot = ((owner & ~1) | core) * CAP + ((owner & 1) ^ core)
        code = jnp.round((amplitudes_ref[position] - AMP_MID) * (1.0 / AMP_STEP))
        out_ref[slot, :N, :] = code.astype(I32).astype(jnp.int16)
        line = jnp.where(lane == 0, offsets_ref[0, position], -1)
        line = jnp.where(lane == 1, offsets_ref[1, position], line)
        out_ref[slot, N:, :] = line.astype(jnp.int16)
        return carry

    lax.fori_loop(0, amplitudes_ref.shape[0], place, 0)


def positions_kernel(
    corner_ref, codes_ref, own_re, own_im, mate_re, mate_im, probe_ref,
    rah, ral, lah, lal, rwh, rwl, lwh, lwl,
    own_out, mate_out, probe_out,
    meta, window, patch, high, low, field, inner, back, total, window_sem, out_sem,
):
    n_mate, count = list_live(corner_ref, meta)
    n_groups = (count + UNROLL - 1) // UNROLL
    mate_last = jnp.maximum((n_mate + UNROLL - 1) // UNROLL - 1, 0)

    def window_copies(group, half, start):
        for u in range(UNROLL):
            item = group * UNROLL + u
            row = pl.multiple_of(jnp.minimum(meta[1, item] // 8 * 8, TILE - WIN_ROWS), 8)
            col = pl.multiple_of(jnp.minimum(meta[2, item] // N, 2) * N, N)
            for tile, sources in enumerate(((own_re, own_im), (mate_re, mate_im))):

                @pl.when(meta[3, item] == tile)
                def _(sources=sources, u=u, row=row, col=col):
                    for part, source in enumerate(sources):
                        for side in range(2):
                            place = pl.ds(pl.multiple_of(col + side * N, N), N)
                            copy = pltpu.make_async_copy(
                                source.at[:, pl.ds(row, WIN_ROWS), place],
                                window.at[half, u, part, side],
                                window_sem.at[half, u, part, side],
                            )
                            copy.start() if start else copy.wait()

    def total_copies(tile):
        out = (own_out, mate_out)[tile]
        return [
            pltpu.make_async_copy(
                total.at[tile, pl.ds(2 * layer, 2), side],
                out.at[layer, :, :, pl.ds(side * N, N)],
                out_sem.at[tile, layer, side],
            )
            for layer in range(2)
            for side in range(TILE // N)
        ]

    @pl.when(n_groups > 0)
    def _():
        window_copies(0, 0, True)

    total[...] = jnp.zeros(total.shape, F32)
    probe_out[...] = jnp.zeros(probe_out.shape, F32)
    lane = lax.broadcasted_iota(I32, (N, N), 1)
    lo, hi = pl.ds(0, N), pl.ds(N, N)
    halves = (lo, hi)

    def step(group, carry):
        buffer = lax.rem(group, 2)

        @pl.when(group + 1 < n_groups)
        def _():
            window_copies(group + 1, 1 - buffer, True)

        window_copies(group, buffer, False)
        items = [group * UNROLL + u for u in range(UNROLL)]
        where = []
        for item in items:
            row, col = meta[1, item], meta[2, item]
            first = jnp.minimum(col // N, 2)
            shift = col - first * N
            row_in = row - jnp.minimum(row // 8 * 8, TILE - WIN_ROWS)
            where.append((meta[3, item], row, row_in, first, shift))

        def put(u, r, c, value):
            big, small = split(value)
            high[u, halves[r], halves[c]] = big
            low[u, halves[r], halves[c]] = small

        def cut(u, layer, part):
            def piece():
                _, _, row_in, _, shift = where[u]
                move = lax.rem(N - shift, N)
                near = window[buffer, u, part, 0, layer, pl.ds(row_in, N), :]
                far = window[buffer, u, part, 1, layer, pl.ds(row_in, N), :]
                both = jnp.where(lane < N - shift, pltpu.roll(near, move, 1), pltpu.roll(far, move, 1))
                patch[u, 2 * layer + part] = both.astype(BF16).astype(F32)

            return piece

        def swap_blocks(u, source):
            def piece(r, c):
                return lambda: put(u, r, c, source[u, halves[c], halves[r]])

            return [piece(r, c) for r in range(2) for c in range(2)]

        def times_patch(u, layer, load, sign):
            def piece(m, c):
                def work():
                    p_re, p_im = patch[u, 2 * layer], patch[u, 2 * layer + 1]
                    if c == 0:
                        put(u, m, 0, load(m, 0) * p_re - sign * (load(m, 1) * p_im))
                    else:
                        put(u, m, 1, load(m, 1) * p_re + sign * (load(m, 0) * p_im))

                return work

            return [piece(m, c) for m in range(2) for c in range(2)]

        def residual(u):
            def factor():
                power = sum(field[u, halves[c], halves[m]] ** 2 for c in range(2) for m in range(2))
                code = codes_ref[meta[0, items[u]], :N, :].astype(I32).astype(F32)
                measured = code * AMP_STEP + AMP_MID
                live = meta[4, items[u]].astype(F32)
                inner_factor[u] = (1.0 - measured * lax.rsqrt(power + 1.0)) * live

            def piece(c, m):
                return lambda: put(u, c, m, field[u, halves[c], halves[m]] * inner_factor[u])

            return [factor] + [piece(c, m) for c in range(2) for m in range(2)]

        inner_factor = {}

        def add_patch(u, plane, value):
            tile, row, _, first, shift = where[u]
            moved = pltpu.roll(value.astype(BF16).astype(F32), lax.rem(shift, N), 1)
            here = (tile, plane, first, pl.ds(row, N))
            there = (tile, plane, first + 1, pl.ds(row, N))
            total[here] = total[here] + jnp.where(lane >= shift, moved, 0.0)
            total[there] = total[there] + jnp.where(lane < shift, moved, 0.0)

        def exit_gradient(u):
            def wave(c, m):
                return inner[u, halves[c], halves[m]]

            def wake(c, m):
                return back[u, halves[m], halves[c]]

            return [
                lambda: add_patch(
                    u, 2, sum(wave(0, m) * wake(0, m) + wave(1, m) * wake(1, m) for m in range(2))
                ),
                lambda: add_patch(
                    u, 3, sum(wave(0, m) * wake(1, m) - wave(1, m) * wake(0, m) for m in range(2))
                ),
            ]

        def entry_gradient(u):
            def wake(c, m):
                return field[u, halves[c], halves[m]]

            def probe_term(m):
                def work():
                    p_re, p_im = patch[u, 0], patch[u, 1]
                    probe_out[m, 0] += p_re * wake(0, m) + p_im * wake(1, m)
                    probe_out[m, 1] += p_re * wake(1, m) - p_im * wake(0, m)

                return work

            return [
                probe_term(0),
                probe_term(1),
                lambda: add_patch(
                    u,
                    0,
                    sum(
                        probe_ref[m, 0] * wake(0, m) + probe_ref[m, 1] * wake(1, m) for m in range(2)
                    ),
                ),
                lambda: add_patch(
                    u,
                    1,
                    sum(
                        probe_ref[m, 0] * wake(1, m) - probe_ref[m, 1] * wake(0, m) for m in range(2)
                    ),
                ),
            ]

        def from_probe(u):
            return lambda m, c: probe_ref[m, c]

        def from_inner(u):
            return lambda m, c: inner[u, halves[c], halves[m]]

        def from_back(u):
            return lambda m, c: back[u, halves[m], halves[c]]

        stages = (
            ("right", rah, ral, field, lambda u: [cut(u, 0, 0), cut(u, 0, 1)] + times_patch(u, 0, from_probe(u), 1), lambda u: []),
            ("left", lah, lal, inner, lambda u: swap_blocks(u, field), lambda u: [cut(u, 1, 0), cut(u, 1, 1)]),
            ("right", rwh, rwl, field, lambda u: times_patch(u, 1, from_inner(u), 1), lambda u: []),
            ("left", lwh, lwl, field, lambda u: swap_blocks(u, field), lambda u: []),
            ("left", rwh, rwl, field, residual, lambda u: []),
            ("right", lwh, lwl, back, lambda u: swap_blocks(u, field), lambda u: []),
            ("right", lah, lal, field, lambda u: times_patch(u, 1, from_back(u), -1), lambda u: []),
            ("left", rah, ral, field, lambda u: swap_blocks(u, field), exit_gradient),
        )
        jobs = [(s, u) for s in range(len(stages)) for u in range(UNROLL)]
        for piece in stages[0][4](0):
            piece()
        for at, (s, u) in enumerate(jobs):
            side, table_high, table_low, result, _, beside = stages[s]
            pieces = list(beside(u))
            if at + 1 < len(jobs):
                s_next, u_next = jobs[at + 1]
                pieces = list(stages[s_next][4](u_next)) + pieces
            if s == len(stages) - 1 and u > 0:
                pieces += entry_gradient(u - 1)
            cuts = [(len(pieces) * k + 2) // 3 for k in range(4)]
            big, small = high[u], low[u]
            sums = None
            for k, (data, table) in enumerate(((big, table_high), (small, table_high), (big, table_low))):
                product = dot(data, table[...]) if side == "right" else dot(table[...], data)
                sums = product if sums is None else sums + product
                for piece in pieces[cuts[k] : cuts[k + 1]]:
                    piece()
            result[u] = sums
        for piece in entry_gradient(UNROLL - 1):
            piece()

        @pl.when(group == mate_last)
        def _():
            for copy in total_copies(1):
                copy.start()

        return carry

    lax.fori_loop(0, n_groups, step, 0)

    @pl.when(n_groups == 0)
    def _():
        for copy in total_copies(1):
            copy.start()

    for copy in total_copies(0):
        copy.start()
    for copy in total_copies(0) + total_copies(1):
        copy.wait()


def spec(space):
    return pl.BlockSpec(memory_space=space)


VMEM, SMEM, ANY = spec(pltpu.VMEM), spec(pltpu.SMEM), spec(pl.ANY)
PARAMS = pltpu.CompilerParams(vmem_limit_bytes=VMEM_LIMIT)
TWO = 2 * N


def run_positions(corners, codes, own_re, own_im, mate_re, mate_im, probe, tables):
    slots = codes.shape[0]
    grad_shape = jax.ShapeDtypeStruct((2, 2, TILE, TILE), F32)
    wave = pltpu.VMEM((UNROLL, TWO, TWO), F32)
    half = pltpu.VMEM((UNROLL, TWO, TWO), BF16)
    return pl.pallas_call(
        positions_kernel,
        out_shape=(grad_shape, grad_shape, jax.ShapeDtypeStruct((2, 2, N, N), F32)),
        in_specs=[SMEM, VMEM] + [ANY] * 4 + [VMEM] * 9,
        out_specs=(ANY, ANY, VMEM),
        scratch_shapes=[
            pltpu.SMEM((5, slots + UNROLL), I32),
            pltpu.VMEM((2, UNROLL, 2, 2, 2, WIN_ROWS, N), F32),
            pltpu.VMEM((UNROLL, 4, N, N), F32),
            half,
            half,
            wave,
            wave,
            wave,
            pltpu.VMEM((2, 4, TILE // N, TILE, N), F32),
            pltpu.SemaphoreType.DMA((2, UNROLL, 2, 2)),
            pltpu.SemaphoreType.DMA((2, 2, TILE // N)),
        ],
        compiler_params=PARAMS,
        cost_estimate=pl.CostEstimate(
            flops=slots * 48 * TWO**3, bytes_accessed=24 * 2**20, transcendentals=0
        ),
        name="positions",
    )(corners, codes, own_re, own_im, mate_re, mate_im, probe, *tables)


def tie(*values):
    return lax.optimization_barrier(values)


def finish(own_grad, mate_grad, probe_part):
    axes = ("region", "scan")
    devices = lax.axis_size("region") * lax.axis_size("scan")
    chips = devices // 2
    mates = [(i, i ^ 1) for i in range(devices)]
    same_core = [list(range(core, devices, 2)) for core in range(2)]
    core = lax.axis_index("scan") & 1
    halves = probe_part.reshape(2, chips, -1)
    kept = lax.dynamic_index_in_dim(halves, core, 0, False)
    given = lax.dynamic_index_in_dim(halves, 1 - core, 0, False)
    mine = kept + lax.ppermute(given, axes, mates)
    mine, mate_grad = tie(mine, mate_grad)
    other_grad = lax.ppermute(mate_grad, axes, mates)
    pieces = lax.all_to_all(mine, axes, 0, 0, axis_index_groups=same_core, tiled=True)
    piece = jnp.sum(pieces, axis=0, keepdims=True)
    piece, other_grad = tie(piece, other_grad)
    half = lax.all_to_all(
        jnp.broadcast_to(piece, pieces.shape), axes, 0, 0, axis_index_groups=same_core, tiled=True
    )
    object_grad = own_grad + other_grad
    half, object_grad = tie(half, object_grad)
    other = lax.ppermute(half, axes, mates)
    whole = jnp.where(core == 0, jnp.stack([half, other]), jnp.stack([other, half]))
    return object_grad, whole.reshape(probe_part.shape)


def body(object_real, object_imag, probe_modes, amplitudes, offsets, owners):
    groups = lax.axis_size("scan")
    pos_dev = offsets.shape[0]
    slots = groups * CAP
    mates = [(i, i ^ 1) for i in range(groups)]
    tables = [jnp.asarray(t) for t in operator_tables()]
    me = lax.axis_index("scan").astype(I32).reshape(1)

    requests = pl.pallas_call(
        prepare_kernel,
        out_shape=jax.ShapeDtypeStruct((slots, N + TAIL, N), jnp.int16),
        in_specs=[SMEM, SMEM, SMEM, VMEM],
        out_specs=VMEM,
        scratch_shapes=[pltpu.SMEM((groups,), I32)],
        compiler_params=PARAMS,
        name="prepare",
    )(me, owners.reshape(pos_dev), offsets.T, amplitudes)
    arrived = lax.all_to_all(
        requests.reshape(groups, CAP, N + TAIL, N), "scan", 0, 0, tiled=True
    ).reshape(slots, N + TAIL, N)
    mate_real = lax.ppermute(object_real, "scan", mates)
    mate_imag = lax.ppermute(object_imag, "scan", mates)
    corners = arrived[:, N, :2].astype(I32).reshape(2 * slots)
    own_grad, mate_grad, probe_part = run_positions(
        corners, arrived, object_real, object_imag, mate_real, mate_imag, probe_modes, tables
    )
    object_grad, probe_grad = finish(own_grad, mate_grad, probe_part)
    return object_grad, probe_grad / pos_dev


def solution(mesh):
    return jax.shard_map(
        body,
        mesh=mesh,
        in_specs=(
            P(None, "region", "scan"),
            P(None, "region", "scan"),
            P(),
            P(("region", "scan"), None, None),
            P(("region", "scan"), None),
            P(("region", "scan"), None),
        ),
        out_specs=(P(None, None, "region", "scan"), P()),
        check_vma=False,
    )
```

time: 962 us -> 106 us (0.11)
  the two profiles are of different devices: /device:TPU:32 before, /device:TPU:1 now
where the time goes in v2:
time: 106 us
  Pallas kernels  39 us (37%)
  waiting for transfers between devices  21.5 us (20%)
  starting transfers between devices  17.5 us (17%)
  blocking collectives  15.9 us (15%)
  other arithmetic  7.41 us (7%)
  local copies, waits for them, and re-layouts  3.95 us (4%)
    pallas_call x1, Pallas kernels, run_positions(): pl.pallas_call(positions_kernel, out_shape=(grad_shape, grad_shape, jax.S...  36.5 us
    all_to_all x1, waiting for transfers between devices, body(): lax.all_to_all(requests.reshape(groups, CAP, N + TAIL, N), 'scan', 0, 0,...  17.3 us
    all_to_all x1, blocking collectives, finish(): lax.all_to_all(mine, axes, 0, 0, axis_index_groups=same_core, tiled=True)  15.9 us
    all_to_all x1, starting transfers between devices, body(): lax.all_to_all(requests.reshape(groups, CAP, N + TAIL, N), 'scan', 0, 0,...  6.84 us
    add x1, other arithmetic, finish(): object_grad = own_grad + other_grad  6.5 us
    all_to_all x1, starting transfers between devices, finish(): lax.all_to_all(jnp.broadcast_to(piece, pieces.shape), axes, 0, 0, axis_in...  4.87 us
    ppermute x1, starting transfers between devices, finish(): other = lax.ppermute(half, axes, mates)  2.81 us
    pallas_call x1, Pallas kernels, body(): pl.pallas_call(prepare_kernel, out_shape=jax.ShapeDtypeStruct((slots, N +...  2.52 us
  transfers between devices with their start and end apart: 7, of which 4 were waited for; matrix products, arithmetic and copies ran while one was open for 7% of the time, Pallas kernels for 2%

profile of v2, /device:TPU:1, one launch (start us, length us, event | category | flops | bytes accessed | tf_op | source)
XLA Modules:
  0.0 106.1 jit_solution(9108695037847945515)
XLA Ops:
  0.6 1.5 %collective-permute-start = (f32[2,512,512]{2,1,0:T(8,128)}, f32[2,512,512]{2,1,0:T(8,128)S(1)}, u32[]{:S(2)}, u32[]{:S(2)}) collective-permute-start(f32[2,512,512]{2,1,0:T(8,128)} %own_re.1), channel_id=1, source_target_pairs={{0,1},{1,0},{2,3},{3,2},{4,5},{5,4},{6,7},{7,6},{8,9},{9,8},{10,11... | collective-permute-start | bytes 6291464 | tf_op jit(solution)/shard_map/ppermute | solution.py:447
  2.1 0.1 collective-permute-start.1
  2.2 2.5 %prepare.1 = s16[32,144,128]{2,1,0:T(8,128)(2,1)} custom-call(s32[1]{0:T(128)} %bitcast.me_ref, s32[16]{0:T(128)} %bitcast.22, s32[2,16]{1,0:T(2,128)} %bitcast.21, f32[16,128,128]{2,1,0:T(8,128)} %amplitudes_ref.1), custom_call_target="tpu_custom_call" | custom-call | tf_op jit(solution)/shard_map/prepare/pallas_call | solution.py:435
  4.7 6.8 %all-to-all-start = ((s16[16,2,144,128]{3,2,1,0:T(8,128)(2,1)}), s16[16,2,144,128]{3,2,1,0:T(8,128)(2,1)S(1)}, u32[]{:S(2)}, u32[]{:S(2)}) async-start(s16[16,2,144,128]{3,2,1,0:T(8,128)(2,1)} %bitcast.16), calls=%async_computation | async-start | bytes 2359296 | tf_op jit(solution)/shard_map/all_to_all | solution.py:444
  11.6 17.3 %all-to-all-done = s16[16,2,144,128]{3,2,1,0:T(8,128)(2,1)S(1)} async-done(((s16[16,2,144,128]{3,2,1,0:T(8,128)(2,1)}), s16[16,2,144,128]{3,2,1,0:T(8,128)(2,1)S(1)}, u32[]{:S(2)}, u32[]{:S(2)}) %all-to-all-start) | async-done | bytes 1179680 | tf_op jit(solution)/shard_map/all_to_all | solution.py:444
  28.9 0.0 copy-start
  28.9 0.1 fusion.1
  28.9 0.8 reshape.45.corner_ref
  29.7 0.0 collective-permute-done.mate_re
  29.7 0.0 copy-start.1
  29.7 0.0 collective-permute-done.1.mate_im
  29.7 0.2 copy-done
  30.0 1.1 copy-done.1
  31.0 36.5 %positions.1 = (f32[2,2,512,512]{3,2,1,0:T(8,128)}, f32[2,2,512,512]{3,2,1,0:T(8,128)}, f32[2,2,128,128]{3,2,1,0:T(8,128)}) custom-call(s32[64]{0:T(128)} %reshape.45.corner_ref, s16[32,144,128]{2,1,0:T(8,128)(2,1)} %bitcast.18, f32[2,512,512]{2,1,0:T(8,128)} %own_re.1, f32[2,512,512]{2,1,0:T(8,128)} %own_im.1, f32[2,512,512]{2,1,0:T(8,128)} %copy-done.1, ...), custom_call_target="tpu_custom_call" | custom-call | flops 25769803776 | bytes 25165824 | tf_op jit(solution)/shard_map/positions/pallas_call | solution.py:371
  67.6 1.0 reshape.44
  68.6 1.0 collective-permute-start.2
  69.6 1.0 collective-permute-done.2
  70.6 0.4 collective-permute-start.3
  71.0 0.1 all_to_all.16
  71.1 15.9 %all_to_all.23 = f32[64,1,512]{2,1,0:T(1,128)S(1)} all-to-all(f32[64,1,512]{2,1,0:T(1,128)S(1)} %all_to_all.16), channel_id=1, replica_groups={{0,2,4,6,8,10,12,14,16,18,20,22,24,26,28,30,32,34,36,38,40,42,44,46,48,..., dimensions={0} | all-to-all | bytes 262144 | tf_op jit(solution)/shard_map/all_to_all | solution.py:414
  87.0 0.1 reduce_sum.9
  87.2 0.0 collective-permute-done.3
  87.2 0.7 broadcast_in_dim.9
  87.9 4.9 %all-to-all-start.2 = ((f32[64,1,512]{2,1,0:T(1,128)}), f32[64,1,512]{2,1,0:T(1,128)S(1)}, u32[]{:S(2)}, u32[]{:S(2)}) async-start(f32[64,1,512]{2,1,0:T(1,128)} %broadcast_in_dim.9), calls=%async_computation.2 | async-start | bytes 262144 | tf_op jit(solution)/shard_map/all_to_all | solution.py:417
  92.8 6.5 %add.17 = f32[2,2,512,512]{3,2,1,0:T(8,128)} add(f32[2,2,512,512]{3,2,1,0:T(8,128)} %get-tuple-element.16, f32[2,2,512,512]{3,2,1,0:T(8,128)} %collective-permute-done.3) | non-fusion elementwise | flops 1048576 | bytes 12582912 | tf_op jit(solution)/shard_map/add | solution.py:420
  99.3 2.3 %all-to-all-done.2 = f32[64,1,512]{2,1,0:T(1,128)S(1)} async-done(((f32[64,1,512]{2,1,0:T(1,128)}), f32[64,1,512]{2,1,0:T(1,128)S(1)}, u32[]{:S(2)}, u32[]{:S(2)}) %all-to-all-start.2) | async-done | bytes 131104 | tf_op jit(solution)/shard_map/all_to_all | solution.py:417
  101.5 2.8 %collective-permute-start.4 = (f32[64,512]{1,0:T(8,128)S(1)}, f32[64,512]{1,0:T(8,128)S(1)}, u32[]{:S(2)}, u32[]{:S(2)}) collective-permute-start(f32[64,512]{1,0:T(8,128)S(1)} %bitcast.19), channel_id=1, source_target_pairs={{0,1},{1,0},{2,3},{3,2},{4,5},{5,4},{6,7},{7,6},{8,9},{9,8},{10,11... | collective-permute-start | bytes 393224 | tf_op jit(solution)/shard_map/ppermute | solution.py:422
  104.3 1.0 collective-permute-done.4
  105.3 0.7 fusion
  (5 shorter events, 0.1 us)
Async XLA Ops:
  0.6 29.1 %collective-permute-start = (f32[2,512,512]{2,1,0:T(8,128)}, f32[2,512,512]{2,1,0:T(8,128)S(1)}, u32[]{:S(2)}, u32[]{:S(2)}) collective-permute-start(f32[2,512,512]{2,1,0:T(8,128)} %own_re.1), channel_id=1, source_target_pairs={{0,1},{1,0},{2,3},{3,2},{4,5},{5,4},{6,7},{7,6},{8,9},{9,8},{10,11... | collective-permute-start | bytes 6291464 | tf_op jit(solution)/shard_map/ppermute | solution.py:447
  2.1 27.6 %collective-permute-start.1 = (f32[2,512,512]{2,1,0:T(8,128)}, f32[2,512,512]{2,1,0:T(8,128)}, u32[]{:S(2)}, u32[]{:S(2)}) collective-permute-start(f32[2,512,512]{2,1,0:T(8,128)} %own_im.1), channel_id=1, source_target_pairs={{0,1},{1,0},{2,3},{3,2},{4,5},{5,4},{6,7},{7,6},{8,9},{9,8},{10,11... | collective-permute-start | bytes 6291464 | tf_op jit(solution)/shard_map/ppermute | solution.py:448
  4.7 24.1 %all-to-all-start = ((s16[16,2,144,128]{3,2,1,0:T(8,128)(2,1)}), s16[16,2,144,128]{3,2,1,0:T(8,128)(2,1)S(1)}, u32[]{:S(2)}, u32[]{:S(2)}) async-start(s16[16,2,144,128]{3,2,1,0:T(8,128)(2,1)} %bitcast.16), calls=%async_computation | async-start | bytes 2359296 | tf_op jit(solution)/shard_map/all_to_all | solution.py:444
  28.9 1.1 %copy-start = (s16[16,2,144,128]{3,2,1,0:T(8,128)(2,1)}, s16[16,2,144,128]{3,2,1,0:T(8,128)(2,1)S(1)}, u32[]{:S(2)}) copy-start(s16[16,2,144,128]{3,2,1,0:T(8,128)(2,1)S(1)} %all-to-all-done) | copy-start | bytes 3538948
  29.7 1.3 %copy-start.1 = (f32[2,512,512]{2,1,0:T(8,128)}, f32[2,512,512]{2,1,0:T(8,128)S(1)}, u32[]{:S(2)}) copy-start(f32[2,512,512]{2,1,0:T(8,128)S(1)} %collective-permute-done.mate_re) | copy-start | bytes 6291460
  68.6 2.0 %collective-permute-start.2 = (f32[64,512]{1,0:T(8,128)S(1)}, f32[64,512]{1,0:T(8,128)S(1)}, u32[]{:S(2)}, u32[]{:S(2)}) collective-permute-start(f32[64,512]{1,0:T(8,128)S(1)} %dynamic-slice_bitcast_fusion), channel_id=1, source_target_pairs={{0,1},{1,0},{2,3},{3,2},{4,5},{5,4},{6,7},{7,6},{8,9},{9,8},{10,11... | collective-permute-start | bytes 393224 | tf_op jit(solution)/shard_map/ppermute | solution.py:411
  70.6 16.6 %collective-permute-start.3 = (f32[2,2,512,512]{3,2,1,0:T(8,128)}, f32[2,2,512,512]{3,2,1,0:T(8,128)}, u32[]{:S(2)}, u32[]{:S(2)}) collective-permute-start(f32[2,2,512,512]{3,2,1,0:T(8,128)} %get-tuple-element.14), channel_id=1, source_target_pairs={{0,1},{1,0},{2,3},{3,2},{4,5},{5,4},{6,7},{7,6},{8,9},{9,8},{10,11... | collective-permute-start | bytes 12582920 | tf_op jit(solution)/shard_map/ppermute | solution.py:413
  87.9 13.6 %all-to-all-start.2 = ((f32[64,1,512]{2,1,0:T(1,128)}), f32[64,1,512]{2,1,0:T(1,128)S(1)}, u32[]{:S(2)}, u32[]{:S(2)}) async-start(f32[64,1,512]{2,1,0:T(1,128)} %broadcast_in_dim.9), calls=%async_computation.2 | async-start | bytes 262144 | tf_op jit(solution)/shard_map/all_to_all | solution.py:417
  101.5 3.8 %collective-permute-start.4 = (f32[64,512]{1,0:T(8,128)S(1)}, f32[64,512]{1,0:T(8,128)S(1)}, u32[]{:S(2)}, u32[]{:S(2)}) collective-permute-start(f32[64,512]{1,0:T(8,128)S(1)} %bitcast.19), channel_id=1, source_target_pairs={{0,1},{1,0},{2,3},{3,2},{4,5},{5,4},{6,7},{7,6},{8,9},{9,8},{10,11... | collective-permute-start | bytes 393224 | tf_op jit(solution)/shard_map/ppermute | solution.py:422

commit v3 on v2

--- a/solution.py
+++ b/solution.py
@@ -69,19 +69,19 @@
 
 
 def list_live(corner_ref, meta):
-    slots = corner_ref.shape[0] // 2
+    slots = corner_ref.shape[0]
 
     def visit(which):
         def look(source, count):
             slot = source * CAP + which
-            row = corner_ref[2 * slot]
+            row = corner_ref[slot, 0]
             live = (row >= 0).astype(I32)
 
             @pl.when(live == 1)
             def _():
                 meta[0, count] = slot
                 meta[1, count] = row
-                meta[2, count] = corner_ref[2 * slot + 1]
+                meta[2, count] = corner_ref[slot, 1]
                 meta[3, count] = which
                 meta[4, count] = 1
 
@@ -120,11 +120,15 @@
 
 
 def positions_kernel(
-    corner_ref, codes_ref, own_re, own_im, mate_re, mate_im, probe_ref,
-    rah, ral, lah, lal, rwh, rwl, lwh, lwl,
+    corner_ref, codes_ref, own_re, own_im, mate_re, mate_im, probe_in, tables_ref,
     own_out, mate_out, probe_out,
-    meta, window, patch, high, low, field, inner, back, total, window_sem, out_sem,
+    meta, window, code, patch, high, low, field, inner, back, total, tables, probe_ref, probe_total,
+    window_sem, code_sem, out_sem, table_sem, probe_sem,
 ):
+    table_copy = pltpu.make_async_copy(tables_ref, tables, table_sem)
+    table_copy.start()
+    probe_copy = pltpu.make_async_copy(probe_in, probe_ref, probe_sem.at[0])
+    probe_copy.start()
     n_mate, count = list_live(corner_ref, meta)
     n_groups = (count + UNROLL - 1) // UNROLL
     mate_last = jnp.maximum((n_mate + UNROLL - 1) // UNROLL - 1, 0)
@@ -148,6 +152,11 @@
                             )
                             copy.start() if start else copy.wait()
 
+            copy = pltpu.make_async_copy(
+                codes_ref.at[meta[0, item], pl.ds(0, N)], code.at[half, u], code_sem.at[half, u]
+            )
+            copy.start() if start else copy.wait()
+
     def total_copies(tile):
         out = (own_out, mate_out)[tile]
         return [
@@ -165,10 +174,11 @@
         window_copies(0, 0, True)
 
     total[...] = jnp.zeros(total.shape, F32)
-    probe_out[...] = jnp.zeros(probe_out.shape, F32)
+    probe_total[...] = jnp.zeros(probe_total.shape, F32)
     lane = lax.broadcasted_iota(I32, (N, N), 1)
-    lo, hi = pl.ds(0, N), pl.ds(N, N)
-    halves = (lo, hi)
+    halves = (pl.ds(0, N), pl.ds(N, N))
+    table_copy.wait()
+    probe_copy.wait()
 
     def step(group, carry):
         buffer = lax.rem(group, 2)
@@ -225,8 +235,7 @@
         def residual(u):
             def factor():
                 power = sum(field[u, halves[c], halves[m]] ** 2 for c in range(2) for m in range(2))
-                code = codes_ref[meta[0, items[u]], :N, :].astype(I32).astype(F32)
-                measured = code * AMP_STEP + AMP_MID
+                measured = code[buffer, u].astype(I32).astype(F32) * AMP_STEP + AMP_MID
                 live = meta[4, items[u]].astype(F32)
                 inner_factor[u] = (1.0 - measured * lax.rsqrt(power + 1.0)) * live
 
@@ -268,8 +277,8 @@
             def probe_term(m):
                 def work():
                     p_re, p_im = patch[u, 0], patch[u, 1]
-                    probe_out[m, 0] += p_re * wake(0, m) + p_im * wake(1, m)
-                    probe_out[m, 1] += p_re * wake(1, m) - p_im * wake(0, m)
+                    probe_total[m, 0] += p_re * wake(0, m) + p_im * wake(1, m)
+                    probe_total[m, 1] += p_re * wake(1, m) - p_im * wake(0, m)
 
                 return work
 
@@ -302,31 +311,32 @@
             return lambda m, c: back[u, halves[m], halves[c]]
 
         stages = (
-            ("right", rah, ral, field, lambda u: [cut(u, 0, 0), cut(u, 0, 1)] + times_patch(u, 0, from_probe(u), 1), lambda u: []),
-            ("left", lah, lal, inner, lambda u: swap_blocks(u, field), lambda u: [cut(u, 1, 0), cut(u, 1, 1)]),
-            ("right", rwh, rwl, field, lambda u: times_patch(u, 1, from_inner(u), 1), lambda u: []),
-            ("left", lwh, lwl, field, lambda u: swap_blocks(u, field), lambda u: []),
-            ("left", rwh, rwl, field, residual, lambda u: []),
-            ("right", lwh, lwl, back, lambda u: swap_blocks(u, field), lambda u: []),
-            ("right", lah, lal, field, lambda u: times_patch(u, 1, from_back(u), -1), lambda u: []),
-            ("left", rah, ral, field, lambda u: swap_blocks(u, field), exit_gradient),
+            ("right", 0, field, lambda u: [cut(u, 0, 0), cut(u, 0, 1)] + times_patch(u, 0, from_probe(u), 1), lambda u: []),
+            ("left", 1, inner, lambda u: swap_blocks(u, field), lambda u: [cut(u, 1, 0), cut(u, 1, 1)]),
+            ("right", 2, field, lambda u: times_patch(u, 1, from_inner(u), 1), lambda u: []),
+            ("left", 3, field, lambda u: swap_blocks(u, field), lambda u: []),
+            ("left", 2, field, residual, lambda u: []),
+            ("right", 3, back, lambda u: swap_blocks(u, field), lambda u: []),
+            ("right", 1, field, lambda u: times_patch(u, 1, from_back(u), -1), lambda u: []),
+            ("left", 0, field, lambda u: swap_blocks(u, field), exit_gradient),
         )
         jobs = [(s, u) for s in range(len(stages)) for u in range(UNROLL)]
-        for piece in stages[0][4](0):
+        for piece in stages[0][3](0):
             piece()
         for at, (s, u) in enumerate(jobs):
-            side, table_high, table_low, result, _, beside = stages[s]
+            side, form, result, _, beside = stages[s]
             pieces = list(beside(u))
             if at + 1 < len(jobs):
                 s_next, u_next = jobs[at + 1]
-                pieces = list(stages[s_next][4](u_next)) + pieces
+                pieces = list(stages[s_next][3](u_next)) + pieces
             if s == len(stages) - 1 and u > 0:
                 pieces += entry_gradient(u - 1)
             cuts = [(len(pieces) * k + 2) // 3 for k in range(4)]
             big, small = high[u], low[u]
             sums = None
-            for k, (data, table) in enumerate(((big, table_high), (small, table_high), (big, table_low))):
-                product = dot(data, table[...]) if side == "right" else dot(table[...], data)
+            for k, (data, part) in enumerate(((big, 0), (small, 0), (big, 1))):
+                table = tables[2 * form + part]
+                product = dot(data, table) if side == "right" else dot(table, data)
                 sums = product if sums is None else sums + product
                 for piece in pieces[cuts[k] : cuts[k + 1]]:
                     piece()
@@ -348,9 +358,10 @@
         for copy in total_copies(1):
             copy.start()
 
-    for copy in total_copies(0):
+    probe_back = pltpu.make_async_copy(probe_total, probe_out, probe_sem.at[1])
+    for copy in total_copies(0) + [probe_back]:
         copy.start()
-    for copy in total_copies(0) + total_copies(1):
+    for copy in total_copies(0) + total_copies(1) + [probe_back]:
         copy.wait()
 
 
@@ -358,7 +369,7 @@
     return pl.BlockSpec(memory_space=space)
 
 
-VMEM, SMEM, ANY = spec(pltpu.VMEM), spec(pltpu.SMEM), spec(pl.ANY)
+VMEM, SMEM, HBM, ANY = spec(pltpu.VMEM), spec(pltpu.SMEM), spec(pltpu.HBM), spec(pl.ANY)
 PARAMS = pltpu.CompilerParams(vmem_limit_bytes=VMEM_LIMIT)
 TWO = 2 * N
 
@@ -371,11 +382,12 @@
     return pl.pallas_call(
         positions_kernel,
         out_shape=(grad_shape, grad_shape, jax.ShapeDtypeStruct((2, 2, N, N), F32)),
-        in_specs=[SMEM, VMEM] + [ANY] * 4 + [VMEM] * 9,
-        out_specs=(ANY, ANY, VMEM),
+        in_specs=[SMEM] + [ANY] * 3 + [HBM] * 2 + [ANY] * 2,
+        out_specs=(ANY, ANY, ANY),
         scratch_shapes=[
             pltpu.SMEM((5, slots + UNROLL), I32),
             pltpu.VMEM((2, UNROLL, 2, 2, 2, WIN_ROWS, N), F32),
+            pltpu.VMEM((2, UNROLL, N, N), jnp.int16),
             pltpu.VMEM((UNROLL, 4, N, N), F32),
             half,
             half,
@@ -383,44 +395,39 @@
             wave,
             wave,
             pltpu.VMEM((2, 4, TILE // N, TILE, N), F32),
+            pltpu.VMEM((8, TWO, TWO), BF16),
+            pltpu.VMEM((2, 2, N, N), F32),
+            pltpu.VMEM((2, 2, N, N), F32),
             pltpu.SemaphoreType.DMA((2, UNROLL, 2, 2)),
+            pltpu.SemaphoreType.DMA((2, UNROLL)),
             pltpu.SemaphoreType.DMA((2, 2, TILE // N)),
+            pltpu.SemaphoreType.DMA,
+            pltpu.SemaphoreType.DMA((2,)),
         ],
         compiler_params=PARAMS,
         cost_estimate=pl.CostEstimate(
             flops=slots * 48 * TWO**3, bytes_accessed=24 * 2**20, transcendentals=0
         ),
         name="positions",
-    )(corners, codes, own_re, own_im, mate_re, mate_im, probe, *tables)
+    )(corners, codes, own_re, own_im, mate_re, mate_im, probe, tables)
 
 
 def tie(*values):
     return lax.optimization_barrier(values)
 
 
-def finish(own_grad, mate_grad, probe_part):
+def finish(own_grad, mate_grad, probe_part, pos_dev):
     axes = ("region", "scan")
     devices = lax.axis_size("region") * lax.axis_size("scan")
-    chips = devices // 2
     mates = [(i, i ^ 1) for i in range(devices)]
-    same_core = [list(range(core, devices, 2)) for core in range(2)]
-    core = lax.axis_index("scan") & 1
-    halves = probe_part.reshape(2, chips, -1)
-    kept = lax.dynamic_index_in_dim(halves, core, 0, False)
-    given = lax.dynamic_index_in_dim(halves, 1 - core, 0, False)
-    mine = kept + lax.ppermute(given, axes, mates)
-    mine, mate_grad = tie(mine, mate_grad)
     other_grad = lax.ppermute(mate_grad, axes, mates)
-    pieces = lax.all_to_all(mine, axes, 0, 0, axis_index_groups=same_core, tiled=True)
-    piece = jnp.sum(pieces, axis=0, keepdims=True)
+    parts = probe_part.reshape(devices, -1, N)
+    pieces = lax.all_to_all(parts, axes, 0, 0, tiled=True)
+    piece = jnp.sum(pieces, axis=0, keepdims=True) / pos_dev
     piece, other_grad = tie(piece, other_grad)
-    half = lax.all_to_all(
-        jnp.broadcast_to(piece, pieces.shape), axes, 0, 0, axis_index_groups=same_core, tiled=True
-    )
+    whole = lax.all_to_all(jnp.broadcast_to(piece, parts.shape), axes, 0, 0, tiled=True)
     object_grad = own_grad + other_grad
-    half, object_grad = tie(half, object_grad)
-    other = lax.ppermute(half, axes, mates)
-    whole = jnp.where(core == 0, jnp.stack([half, other]), jnp.stack([other, half]))
+    whole, object_grad = tie(whole, object_grad)
     return object_grad, whole.reshape(probe_part.shape)
 
 
@@ -429,7 +436,7 @@
     pos_dev = offsets.shape[0]
     slots = groups * CAP
     mates = [(i, i ^ 1) for i in range(groups)]
-    tables = [jnp.asarray(t) for t in operator_tables()]
+    tables = jnp.asarray(np.stack(operator_tables()))
     me = lax.axis_index("scan").astype(I32).reshape(1)
 
     requests = pl.pallas_call(
@@ -446,12 +453,11 @@
     ).reshape(slots, N + TAIL, N)
     mate_real = lax.ppermute(object_real, "scan", mates)
     mate_imag = lax.ppermute(object_imag, "scan", mates)
-    corners = arrived[:, N, :2].astype(I32).reshape(2 * slots)
+    corners = arrived[:, N, :2].astype(I32)
     own_grad, mate_grad, probe_part = run_positions(
         corners, arrived, object_real, object_imag, mate_real, mate_imag, probe_modes, tables
     )
-    object_grad, probe_grad = finish(own_grad, mate_grad, probe_part)
-    return object_grad, probe_grad / pos_dev
+    return finish(own_grad, mate_grad, probe_part, pos_dev)
 
 
 def solution(mesh):

time: 106 us -> 103 us (0.972)
  blocking collectives: 15.9 us -> 42.5 us
  waiting for transfers between devices: 21.5 us -> 5.06 us
  starting transfers between devices: 17.5 us -> 6.1 us
  local copies, waits for them, and re-layouts: 3.95 us -> 2.75 us
    all_to_all x1 -> x2, blocking collectives: 15.9 us -> 42.5 us  [the longest x1 24.2 us: body(): lax.all_to_all(requests.reshape(groups, CAP, N + TAIL, N), 'scan', 0, 0,...]
    all_to_all x2 -> x1, waiting for transfers between devices: 19.5 us -> 5.05 us  [finish(): lax.all_to_all(jnp.broadcast_to(piece, parts.shape), axes, 0, 0, tiled=True)]
    all_to_all x2 -> x1, starting transfers between devices: 11.7 us -> 3.86 us  [finish(): lax.all_to_all(jnp.broadcast_to(piece, parts.shape), axes, 0, 0, tiled=True)]
    ppermute x2 -> x0, starting transfers between devices: 3.81 us -> none  [the longest x1 2.81 us: finish(): other = lax.ppermute(half, axes, mates)]
    ppermute x2 -> x0, waiting for transfers between devices: 1.96 us -> none  [the longest x1 0.99 us: finish(): mine = kept + lax.ppermute(given, axes, mates)]
  transfers between devices with their start and end apart: 7 -> 4, of which waited for: 4 -> 1; matrix products, arithmetic and copies ran while one was open for 7% -> 7% of each run, Pallas kernels for 2% -> 2%
where the time goes in v3:
time: 103 us
  blocking collectives  42.5 us (41%)
  Pallas kernels  38.2 us (37%)
  other arithmetic  7.32 us (7%)
  starting transfers between devices  6.1 us (6%)
  waiting for transfers between devices  5.06 us (5%)
  local copies, waits for them, and re-layouts  2.75 us (3%)
    pallas_call x1, Pallas kernels, run_positions(): pl.pallas_call(positions_kernel, out_shape=(grad_shape, grad_shape, jax.S...  35.7 us
    all_to_all x1, blocking collectives, body(): lax.all_to_all(requests.reshape(groups, CAP, N + TAIL, N), 'scan', 0, 0,...  24.2 us
    all_to_all x1, blocking collectives, finish(): pieces = lax.all_to_all(parts, axes, 0, 0, tiled=True)  18.3 us
    add x1, other arithmetic, finish(): object_grad = own_grad + other_grad  6.5 us
    all_to_all x1, waiting for transfers between devices, finish(): lax.all_to_all(jnp.broadcast_to(piece, parts.shape), axes, 0, 0, tiled=True)  5.05 us
    all_to_all x1, starting transfers between devices, finish(): lax.all_to_all(jnp.broadcast_to(piece, parts.shape), axes, 0, 0, tiled=True)  3.86 us
    pallas_call x1, Pallas kernels, body(): pl.pallas_call(prepare_kernel, out_shape=jax.ShapeDtypeStruct((slots, N +...  2.52 us
  transfers between devices with their start and end apart: 4, of which 1 were waited for; matrix products, arithmetic and copies ran while one was open for 7% of the time, Pallas kernels for 2%

profile of v3, /device:TPU:1, one launch (start us, length us, event | category | flops | bytes accessed | tf_op | source)
XLA Modules:
  0.0 102.6 jit_solution(9217565895946281280)
XLA Ops:
  0.6 1.5 %collective-permute-start = (f32[2,512,512]{2,1,0:T(8,128)}, f32[2,512,512]{2,1,0:T(8,128)S(1)}, u32[]{:S(2)}, u32[]{:S(2)}) collective-permute-start(f32[2,512,512]{2,1,0:T(8,128)} %own_re.1), channel_id=1, source_target_pairs={{0,1},{1,0},{2,3},{3,2},{4,5},{5,4},{6,7},{7,6},{8,9},{9,8},{10,11... | collective-permute-start | bytes 6291464 | tf_op jit(solution)/shard_map/ppermute | solution.py:454
  2.1 0.1 collective-permute-start.1
  2.2 2.5 %prepare.1 = s16[32,144,128]{2,1,0:T(8,128)(2,1)} custom-call(s32[1]{0:T(128)} %bitcast.me_ref, s32[16]{0:T(128)} %bitcast.19, s32[2,16]{1,0:T(2,128)} %bitcast.18, f32[16,128,128]{2,1,0:T(8,128)} %amplitudes_ref.1), custom_call_target="tpu_custom_call" | custom-call | tf_op jit(solution)/shard_map/prepare/pallas_call | solution.py:442
  4.7 24.2 %all_to_all.15 = s16[16,2,144,128]{3,2,1,0:T(8,128)(2,1)S(1)} all-to-all(s16[16,2,144,128]{3,2,1,0:T(8,128)(2,1)} %bitcast.11), channel_id=1, replica_groups=mesh['region'=8,'scan'=16] {'scan'}, dimensions={0} | all-to-all | bytes 2359296 | tf_op jit(solution)/shard_map/all_to_all | solution.py:451
  29.0 0.0 copy-start
  29.0 0.7 slice_convert_fusion
  29.6 0.0 collective-permute-done.mate_re
  29.6 0.0 copy-start.1
  29.6 0.0 collective-permute-done.1.mate_im
  29.6 0.4 copy-done
  30.1 0.9 copy-done.1
  31.0 35.7 %positions.1 = (f32[2,2,512,512]{3,2,1,0:T(8,128)}, f32[2,2,512,512]{3,2,1,0:T(8,128)}, f32[2,2,128,128]{3,2,1,0:T(8,128)}) custom-call(s32[32,2]{1,0:T(8,128)} %bitcast.16, s16[32,144,128]{2,1,0:T(8,128)(2,1)} %bitcast.13, f32[2,512,512]{2,1,0:T(8,128)} %own_re.1, f32[2,512,512]{2,1,0:T(8,128)} %own_im.1, f32[2,512,512]{2,1,0:T(8,128)} %copy-done.1, ...), custom_call_target="tpu_custom_call" | custom-call | flops 25769803776 | bytes 25165824 | tf_op jit(solution)/shard_map/positions/pallas_call | solution.py:382
  66.7 0.6 collective-permute-start.2
  67.3 18.3 %all_to_all.16 = f32[128,4,128]{2,1,0:T(4,128)S(1)} all-to-all(f32[128,4,128]{2,1,0:T(4,128)} %bitcast.15), channel_id=1, replica_groups=mesh['region'=8,'scan'=16] {'region','scan'}, dimensions={0} | all-to-all | bytes 524288 | tf_op jit(solution)/shard_map/all_to_all | solution.py:425
  85.6 0.1 reduce_sum.9
  85.8 0.0 collective-permute-done.2
  85.8 0.7 broadcast_in_dim.9
  86.5 3.9 %all-to-all-start.2 = ((f32[128,4,128]{2,1,0:T(4,128)}), f32[128,4,128]{2,1,0:T(4,128)S(1)}, u32[]{:S(2)}, u32[]{:S(2)}) async-start(f32[128,4,128]{2,1,0:T(4,128)} %broadcast_in_dim.9), calls=%async_computation.2 | async-start | bytes 524288 | tf_op jit(solution)/shard_map/all_to_all | solution.py:428
  90.4 6.5 %add.3 = f32[2,2,512,512]{3,2,1,0:T(8,128)} add(f32[2,2,512,512]{3,2,1,0:T(8,128)} %get-tuple-element.12, f32[2,2,512,512]{3,2,1,0:T(8,128)} %collective-permute-done.2) | non-fusion elementwise | flops 1048576 | bytes 12582912 | tf_op jit(solution)/shard_map/add | solution.py:429
  96.9 5.1 %all-to-all-done.2 = f32[128,4,128]{2,1,0:T(4,128)S(1)} async-done(((f32[128,4,128]{2,1,0:T(4,128)}), f32[128,4,128]{2,1,0:T(4,128)S(1)}, u32[]{:S(2)}, u32[]{:S(2)}) %all-to-all-start.2) | async-done | bytes 262176 | tf_op jit(solution)/shard_map/all_to_all | solution.py:428
  101.9 0.7 copy.15
  (1 shorter events, 0.0 us)
Async XLA Ops:
  0.6 29.0 %collective-permute-start = (f32[2,512,512]{2,1,0:T(8,128)}, f32[2,512,512]{2,1,0:T(8,128)S(1)}, u32[]{:S(2)}, u32[]{:S(2)}) collective-permute-start(f32[2,512,512]{2,1,0:T(8,128)} %own_re.1), channel_id=1, source_target_pairs={{0,1},{1,0},{2,3},{3,2},{4,5},{5,4},{6,7},{7,6},{8,9},{9,8},{10,11... | collective-permute-start | bytes 6291464 | tf_op jit(solution)/shard_map/ppermute | solution.py:454
  2.1 27.5 %collective-permute-start.1 = (f32[2,512,512]{2,1,0:T(8,128)}, f32[2,512,512]{2,1,0:T(8,128)}, u32[]{:S(2)}, u32[]{:S(2)}) collective-permute-start(f32[2,512,512]{2,1,0:T(8,128)} %own_im.1), channel_id=1, source_target_pairs={{0,1},{1,0},{2,3},{3,2},{4,5},{5,4},{6,7},{7,6},{8,9},{9,8},{10,11... | collective-permute-start | bytes 6291464 | tf_op jit(solution)/shard_map/ppermute | solution.py:455
  29.0 1.1 %copy-start = (s16[16,2,144,128]{3,2,1,0:T(8,128)(2,1)}, s16[16,2,144,128]{3,2,1,0:T(8,128)(2,1)S(1)}, u32[]{:S(2)}) copy-start(s16[16,2,144,128]{3,2,1,0:T(8,128)(2,1)S(1)} %all_to_all.15) | copy-start | bytes 3538948
  29.6 1.3 %copy-start.1 = (f32[2,512,512]{2,1,0:T(8,128)}, f32[2,512,512]{2,1,0:T(8,128)S(1)}, u32[]{:S(2)}) copy-start(f32[2,512,512]{2,1,0:T(8,128)S(1)} %collective-permute-done.mate_re) | copy-start | bytes 6291460
  66.7 19.1 %collective-permute-start.2 = (f32[2,2,512,512]{3,2,1,0:T(8,128)}, f32[2,2,512,512]{3,2,1,0:T(8,128)}, u32[]{:S(2)}, u32[]{:S(2)}) collective-permute-start(f32[2,2,512,512]{3,2,1,0:T(8,128)} %get-tuple-element.10), channel_id=1, source_target_pairs={{0,1},{1,0},{2,3},{3,2},{4,5},{5,4},{6,7},{7,6},{8,9},{9,8},{10,11... | collective-permute-start | bytes 12582920 | tf_op jit(solution)/shard_map/ppermute | solution.py:423
  86.5 15.4 %all-to-all-start.2 = ((f32[128,4,128]{2,1,0:T(4,128)}), f32[128,4,128]{2,1,0:T(4,128)S(1)}, u32[]{:S(2)}, u32[]{:S(2)}) async-start(f32[128,4,128]{2,1,0:T(4,128)} %broadcast_in_dim.9), calls=%async_computation.2 | async-start | bytes 524288 | tf_op jit(solution)/shard_map/all_to_all | solution.py:428

commit v4 on v3

--- a/solution.py
+++ b/solution.py
@@ -119,61 +119,53 @@
     lax.fori_loop(0, amplitudes_ref.shape[0], place, 0)
 
 
+def round_kernel(own_re, own_im, mate_re, mate_im, out_ref):
+    for tile, sources in enumerate(((own_re, own_im), (mate_re, mate_im))):
+
+        @pl.when(pl.program_id(0) == tile)
+        def _(sources=sources):
+            for part, source in enumerate(sources):
+                out_ref[0, 0, part] = source[...].astype(BF16).astype(F32)
+
+
 def positions_kernel(
-    corner_ref, codes_ref, own_re, own_im, mate_re, mate_im, probe_in, tables_ref,
-    own_out, mate_out, probe_out,
-    meta, window, code, patch, high, low, field, inner, back, total, tables, probe_ref, probe_total,
+    corner_ref, codes_ref, tiles_ref, probe_in, tables_ref,
+    grad_out, probe_out,
+    meta, window, code, patch, high, low, field, inner, back, grad, tables, probe_ref, probe_total,
     window_sem, code_sem, out_sem, table_sem, probe_sem,
 ):
     table_copy = pltpu.make_async_copy(tables_ref, tables, table_sem)
     table_copy.start()
     probe_copy = pltpu.make_async_copy(probe_in, probe_ref, probe_sem.at[0])
     probe_copy.start()
-    n_mate, count = list_live(corner_ref, meta)
+    _, count = list_live(corner_ref, meta)
     n_groups = (count + UNROLL - 1) // UNROLL
-    mate_last = jnp.maximum((n_mate + UNROLL - 1) // UNROLL - 1, 0)
 
     def window_copies(group, half, start):
         for u in range(UNROLL):
             item = group * UNROLL + u
             row = pl.multiple_of(jnp.minimum(meta[1, item] // 8 * 8, TILE - WIN_ROWS), 8)
-            col = pl.multiple_of(jnp.minimum(meta[2, item] // N, 2) * N, N)
-            for tile, sources in enumerate(((own_re, own_im), (mate_re, mate_im))):
-
-                @pl.when(meta[3, item] == tile)
-                def _(sources=sources, u=u, row=row, col=col):
-                    for part, source in enumerate(sources):
-                        for side in range(2):
-                            place = pl.ds(pl.multiple_of(col + side * N, N), N)
-                            copy = pltpu.make_async_copy(
-                                source.at[:, pl.ds(row, WIN_ROWS), place],
-                                window.at[half, u, part, side],
-                                window_sem.at[half, u, part, side],
-                            )
-                            copy.start() if start else copy.wait()
-
+            col = jnp.minimum(meta[2, item] // N, 2)
+            copy = pltpu.make_async_copy(
+                tiles_ref.at[meta[3, item], pl.ds(col, 2), :, :, pl.ds(row, WIN_ROWS)],
+                window.at[half, u],
+                window_sem.at[half, u],
+            )
+            copy.start() if start else copy.wait()
             copy = pltpu.make_async_copy(
                 codes_ref.at[meta[0, item], pl.ds(0, N)], code.at[half, u], code_sem.at[half, u]
             )
             copy.start() if start else copy.wait()
 
-    def total_copies(tile):
-        out = (own_out, mate_out)[tile]
-        return [
-            pltpu.make_async_copy(
-                total.at[tile, pl.ds(2 * layer, 2), side],
-                out.at[layer, :, :, pl.ds(side * N, N)],
-                out_sem.at[tile, layer, side],
-            )
-            for layer in range(2)
-            for side in range(TILE // N)
-        ]
+    def grad_copy(group, half):
+        return pltpu.make_async_copy(
+            grad.at[half], grad_out.at[pl.ds(group * UNROLL, UNROLL)], out_sem.at[half]
+        )
 
     @pl.when(n_groups > 0)
     def _():
         window_copies(0, 0, True)
 
-    total[...] = jnp.zeros(total.shape, F32)
     probe_total[...] = jnp.zeros(probe_total.shape, F32)
     lane = lax.broadcasted_iota(I32, (N, N), 1)
     halves = (pl.ds(0, N), pl.ds(N, N))
@@ -188,14 +180,18 @@
             window_copies(group + 1, 1 - buffer, True)
 
         window_copies(group, buffer, False)
+
+        @pl.when(group >= 2)
+        def _():
+            grad_copy(group - 2, buffer).wait()
+
         items = [group * UNROLL + u for u in range(UNROLL)]
         where = []
         for item in items:
             row, col = meta[1, item], meta[2, item]
-            first = jnp.minimum(col // N, 2)
-            shift = col - first * N
+            shift = col - jnp.minimum(col // N, 2) * N
             row_in = row - jnp.minimum(row // 8 * 8, TILE - WIN_ROWS)
-            where.append((meta[3, item], row, row_in, first, shift))
+            where.append((row_in, shift))
 
         def put(u, r, c, value):
             big, small = split(value)
@@ -204,12 +200,12 @@
 
         def cut(u, layer, part):
             def piece():
-                _, _, row_in, _, shift = where[u]
+                row_in, shift = where[u]
                 move = lax.rem(N - shift, N)
-                near = window[buffer, u, part, 0, layer, pl.ds(row_in, N), :]
-                far = window[buffer, u, part, 1, layer, pl.ds(row_in, N), :]
+                near = window[buffer, u, 0, part, layer, pl.ds(row_in, N), :]
+                far = window[buffer, u, 1, part, layer, pl.ds(row_in, N), :]
                 both = jnp.where(lane < N - shift, pltpu.roll(near, move, 1), pltpu.roll(far, move, 1))
-                patch[u, 2 * layer + part] = both.astype(BF16).astype(F32)
+                patch[u, 2 * layer + part] = both
 
             return piece
 
@@ -247,12 +243,7 @@
         inner_factor = {}
 
         def add_patch(u, plane, value):
-            tile, row, _, first, shift = where[u]
-            moved = pltpu.roll(value.astype(BF16).astype(F32), lax.rem(shift, N), 1)
-            here = (tile, plane, first, pl.ds(row, N))
-            there = (tile, plane, first + 1, pl.ds(row, N))
-            total[here] = total[here] + jnp.where(lane >= shift, moved, 0.0)
-            total[there] = total[there] + jnp.where(lane < shift, moved, 0.0)
+            grad[buffer, u, plane] = value.astype(BF16)
 
         def exit_gradient(u):
             def wave(c, m):
@@ -344,6 +335,70 @@
         for piece in entry_gradient(UNROLL - 1):
             piece()
 
+        grad_copy(group, buffer).start()
+        return carry
+
+    lax.fori_loop(0, n_groups, step, 0)
+    probe_back = pltpu.make_async_copy(probe_total, probe_out, probe_sem.at[1])
+    probe_back.start()
+    for before in (2, 1):
+
+        @pl.when(n_groups >= before)
+        def _(before=before):
+            grad_copy(n_groups - before, lax.rem(n_groups - before, 2)).wait()
+
+    probe_back.wait()
+
+
+def scatter_kernel(corner_ref, grad_in, own_out, mate_out, meta, grad, total, in_sem, out_sem):
+    n_mate, count = list_live(corner_ref, meta)
+    n_groups = (count + UNROLL - 1) // UNROLL
+    mate_last = jnp.maximum((n_mate + UNROLL - 1) // UNROLL - 1, 0)
+
+    def grad_copy(group, half):
+        return pltpu.make_async_copy(
+            grad_in.at[pl.ds(group * UNROLL, UNROLL)], grad.at[half], in_sem.at[half]
+        )
+
+    def total_copies(tile):
+        out = (own_out, mate_out)[tile]
+        return [
+            pltpu.make_async_copy(
+                total.at[tile, pl.ds(2 * layer, 2), side],
+                out.at[layer, :, :, pl.ds(side * N, N)],
+                out_sem.at[tile, layer, side],
+            )
+            for layer in range(2)
+            for side in range(TILE // N)
+        ]
+
+    @pl.when(n_groups > 0)
+    def _():
+        grad_copy(0, 0).start()
+
+    total[...] = jnp.zeros(total.shape, F32)
+    lane = lax.broadcasted_iota(I32, (N, N), 1)
+
+    def step(group, carry):
+        half = lax.rem(group, 2)
+
+        @pl.when(group + 1 < n_groups)
+        def _():
+            grad_copy(group + 1, 1 - half).start()
+
+        grad_copy(group, half).wait()
+        for u in range(UNROLL):
+            item = group * UNROLL + u
+            row, col, tile = meta[1, item], meta[2, item], meta[3, item]
+            first = jnp.minimum(col // N, 2)
+            shift = col - first * N
+            for plane in range(4):
+                moved = pltpu.roll(grad[half, u, plane].astype(F32), lax.rem(shift, N), 1)
+                here = (tile, plane, first, pl.ds(row, N))
+                there = (tile, plane, first + 1, pl.ds(row, N))
+                total[here] = total[here] + jnp.where(lane >= shift, moved, 0.0)
+                total[there] = total[there] + jnp.where(lane < shift, moved, 0.0)
+
         @pl.when(group == mate_last)
         def _():
             for copy in total_copies(1):
@@ -358,10 +413,9 @@
         for copy in total_copies(1):
             copy.start()
 
-    probe_back = pltpu.make_async_copy(probe_total, probe_out, probe_sem.at[1])
-    for copy in total_copies(0) + [probe_back]:
+    for copy in total_copies(0):
         copy.start()
-    for copy in total_copies(0) + total_copies(1) + [probe_back]:
+    for copy in total_copies(0) + total_copies(1):
         copy.wait()
 
 
@@ -374,16 +428,38 @@
 TWO = 2 * N
 
 
-def run_positions(corners, codes, own_re, own_im, mate_re, mate_im, probe, tables):
+def run_round(own_re, own_im, mate_re, mate_im):
+    strips = TILE // N
+
+    def index_of(tile):
+        idle = strips - 1 if tile == 0 else 0
+        return lambda t, strip: (0, 0, jnp.where(t == tile, strip, idle))
+
+    block = (2, TILE, N)
+    return pl.pallas_call(
+        round_kernel,
+        grid=(2, strips),
+        out_shape=jax.ShapeDtypeStruct((2, strips, 2, 2, TILE, N), F32),
+        in_specs=[pl.BlockSpec(block, index_of(tile)) for tile in (0, 0, 1, 1)],
+        out_specs=pl.BlockSpec((1, 1, 2, 2, TILE, N), lambda t, strip: (t, strip, 0, 0, 0, 0)),
+        compiler_params=PARAMS,
+        cost_estimate=pl.CostEstimate(flops=0, bytes_accessed=16 * 2**20, transcendentals=0),
+        name="round",
+    )(own_re, own_im, mate_re, mate_im)
+
+
+def run_positions(corners, codes, tiles, probe, tables):
     slots = codes.shape[0]
-    grad_shape = jax.ShapeDtypeStruct((2, 2, TILE, TILE), F32)
     wave = pltpu.VMEM((UNROLL, TWO, TWO), F32)
     half = pltpu.VMEM((UNROLL, TWO, TWO), BF16)
     return pl.pallas_call(
         positions_kernel,
-        out_shape=(grad_shape, grad_shape, jax.ShapeDtypeStruct((2, 2, N, N), F32)),
-        in_specs=[SMEM] + [ANY] * 3 + [HBM] * 2 + [ANY] * 2,
-        out_specs=(ANY, ANY, ANY),
+        out_shape=(
+            jax.ShapeDtypeStruct((slots, 4, N, N), BF16),
+            jax.ShapeDtypeStruct((2, 2, N, N), F32),
+        ),
+        in_specs=[SMEM] + [ANY] * 4,
+        out_specs=(ANY, ANY),
         scratch_shapes=[
             pltpu.SMEM((5, slots + UNROLL), I32),
             pltpu.VMEM((2, UNROLL, 2, 2, 2, WIN_ROWS, N), F32),
@@ -394,13 +470,13 @@
             wave,
             wave,
             wave,
-            pltpu.VMEM((2, 4, TILE // N, TILE, N), F32),
+            pltpu.VMEM((2, UNROLL, 4, N, N), BF16),
             pltpu.VMEM((8, TWO, TWO), BF16),
             pltpu.VMEM((2, 2, N, N), F32),
             pltpu.VMEM((2, 2, N, N), F32),
-            pltpu.SemaphoreType.DMA((2, UNROLL, 2, 2)),
             pltpu.SemaphoreType.DMA((2, UNROLL)),
-            pltpu.SemaphoreType.DMA((2, 2, TILE // N)),
+            pltpu.SemaphoreType.DMA((2, UNROLL)),
+            pltpu.SemaphoreType.DMA((2,)),
             pltpu.SemaphoreType.DMA,
             pltpu.SemaphoreType.DMA((2,)),
         ],
@@ -409,22 +485,44 @@
             flops=slots * 48 * TWO**3, bytes_accessed=24 * 2**20, transcendentals=0
         ),
         name="positions",
-    )(corners, codes, own_re, own_im, mate_re, mate_im, probe, tables)
+    )(corners, codes, tiles, probe, tables)
+
+
+def run_scatter(corners, grads):
+    slots = grads.shape[0]
+    grad_shape = jax.ShapeDtypeStruct((2, 2, TILE, TILE), F32)
+    return pl.pallas_call(
+        scatter_kernel,
+        out_shape=(grad_shape, grad_shape),
+        in_specs=[SMEM, ANY],
+        out_specs=(ANY, ANY),
+        scratch_shapes=[
+            pltpu.SMEM((5, slots + UNROLL), I32),
+            pltpu.VMEM((2, UNROLL, 4, N, N), BF16),
+            pltpu.VMEM((2, 4, TILE // N, TILE, N), F32),
+            pltpu.SemaphoreType.DMA((2,)),
+            pltpu.SemaphoreType.DMA((2, 2, TILE // N)),
+        ],
+        compiler_params=PARAMS,
+        cost_estimate=pl.CostEstimate(flops=0, bytes_accessed=20 * 2**20, transcendentals=0),
+        name="scatter",
+    )(corners, grads)
 
 
 def tie(*values):
     return lax.optimization_barrier(values)
 
 
-def finish(own_grad, mate_grad, probe_part, pos_dev):
+def finish(corners, grads, probe_part, pos_dev):
     axes = ("region", "scan")
     devices = lax.axis_size("region") * lax.axis_size("scan")
     mates = [(i, i ^ 1) for i in range(devices)]
-    other_grad = lax.ppermute(mate_grad, axes, mates)
     parts = probe_part.reshape(devices, -1, N)
+    own_grad, mate_grad = run_scatter(corners, grads)
     pieces = lax.all_to_all(parts, axes, 0, 0, tiled=True)
     piece = jnp.sum(pieces, axis=0, keepdims=True) / pos_dev
-    piece, other_grad = tie(piece, other_grad)
+    piece, own_grad, mate_grad = tie(piece, own_grad, mate_grad)
+    other_grad = lax.ppermute(mate_grad, axes, mates)
     whole = lax.all_to_all(jnp.broadcast_to(piece, parts.shape), axes, 0, 0, tiled=True)
     object_grad = own_grad + other_grad
     whole, object_grad = tie(whole, object_grad)
@@ -453,11 +551,13 @@
     ).reshape(slots, N + TAIL, N)
     mate_real = lax.ppermute(object_real, "scan", mates)
     mate_imag = lax.ppermute(object_imag, "scan", mates)
+    tiles = run_round(object_real, object_imag, mate_real, mate_imag)
+    arrived, tiles = tie(arrived, tiles)
     corners = arrived[:, N, :2].astype(I32)
-    own_grad, mate_grad, probe_part = run_positions(
-        corners, arrived, object_real, object_imag, mate_real, mate_imag, probe_modes, tables
+    grads, probe_part = run_positions(
+        corners, arrived, tiles, probe_modes, tables
     )
-    return finish(own_grad, mate_grad, probe_part, pos_dev)
+    return finish(corners, grads, probe_part, pos_dev)
 
 
 def solution(mesh):

time: 103 us -> 101 us (0.981); the launches traced: 103 us -> 99.2 us
  blocking collectives: 42.5 us -> 0 us
  starting transfers between devices: 6.1 us -> 31.3 us
  waiting for transfers between devices: 5.06 us -> 15.7 us
  Pallas kernels: 38.2 us -> 41.1 us
    all_to_all x2 -> x0, blocking collectives: 42.5 us -> none  [the longest x1 24.2 us: body(): lax.all_to_all(requests.reshape(groups, CAP, N + TAIL, N), 'scan', 0, 0,...]
    all_to_all x0 -> x2, starting transfers between devices: none -> 22.8 us  [the longest x1 15.9 us: finish(): pieces = lax.all_to_all(parts, axes, 0, 0, tiled=True)]
    all_to_all x0 -> x2, waiting for transfers between devices: none -> 10.7 us  [the longest x1 6.44 us: body(): lax.all_to_all(requests.reshape(groups, CAP, N + TAIL, N), 'scan', 0, 0,...]
    pallas_call x1 -> x3, Pallas kernels: 35.7 us -> 38.6 us  [the longest x1 21.8 us: run_positions(): pl.pallas_call(positions_kernel, out_shape=(jax.ShapeDtypeStruct((slots,...]
    all_to_all x1, starting transfers between devices: 3.86 us -> 6.45 us  [finish(): lax.all_to_all(jnp.broadcast_to(piece, parts.shape), axes, 0, 0, tiled=True)]
  transfers between devices with their start and end apart: 4 -> 6, of which waited for: 1 -> 3; matrix products, arithmetic and copies ran while one was open for 7% -> 7% of each run, Pallas kernels for 2% -> 19%
where the time goes in v4:
time: 101 us; the launch traced here: 99.2 us
  Pallas kernels  41.1 us (41%)
  starting transfers between devices  31.3 us (31%)
  waiting for transfers between devices  15.7 us (16%)
  other arithmetic  7.31 us (7%)
  local copies, waits for them, and re-layouts  3.18 us (3%)
    pallas_call x1, Pallas kernels, run_positions(): pl.pallas_call(positions_kernel, out_shape=(jax.ShapeDtypeStruct((slots,...  21.8 us
    all_to_all x1, starting transfers between devices, finish(): pieces = lax.all_to_all(parts, axes, 0, 0, tiled=True)  15.9 us
    pallas_call x1, Pallas kernels, run_round(): pl.pallas_call(round_kernel, grid=(2, strips), out_shape=jax.ShapeDtypeSt...  9.52 us
    pallas_call x1, Pallas kernels, run_scatter(): pl.pallas_call(scatter_kernel, out_shape=(grad_shape, grad_shape), in_spe...  7.22 us
    all_to_all x1, starting transfers between devices, body(): lax.all_to_all(requests.reshape(groups, CAP, N + TAIL, N), 'scan', 0, 0,...  6.84 us
    add x1, other arithmetic, finish(): object_grad = own_grad + other_grad  6.5 us
    all_to_all x1, starting transfers between devices, finish(): lax.all_to_all(jnp.broadcast_to(piece, parts.shape), axes, 0, 0, tiled=True)  6.45 us
    all_to_all x1, waiting for transfers between devices, body(): lax.all_to_all(requests.reshape(groups, CAP, N + TAIL, N), 'scan', 0, 0,...  6.44 us
  transfers between devices with their start and end apart: 6, of which 3 were waited for; matrix products, arithmetic and copies ran while one was open for 7% of the time, Pallas kernels for 19%

profile of v4, /device:TPU:1, one launch (start us, length us, event | category | flops | bytes accessed | tf_op | source)
XLA Modules:
  0.0 99.2 jit_solution(12360799218827621860)
XLA Ops:
  0.6 1.5 %collective-permute-start = (f32[2,512,512]{2,1,0:T(8,128)}, f32[2,512,512]{2,1,0:T(8,128)S(1)}, u32[]{:S(2)}, u32[]{:S(2)}) collective-permute-start(f32[2,512,512]{2,1,0:T(8,128)} %own_re.1), channel_id=1, source_target_pairs={{0,1},{1,0},{2,3},{3,2},{4,5},{5,4},{6,7},{7,6},{8,9},{9,8},{10,11... | collective-permute-start | bytes 6291464 | tf_op jit(solution)/shard_map/ppermute | solution.py:552
  2.1 0.1 collective-permute-start.1
  2.2 2.5 %prepare.1 = s16[32,144,128]{2,1,0:T(8,128)(2,1)} custom-call(s32[1]{0:T(128)} %bitcast.me_ref, s32[16]{0:T(128)} %bitcast.20, s32[2,16]{1,0:T(2,128)} %bitcast.19, f32[16,128,128]{2,1,0:T(8,128)} %amplitudes_ref.1), custom_call_target="tpu_custom_call" | custom-call | tf_op jit(solution)/shard_map/prepare/pallas_call | solution.py:540
  4.8 6.8 %all-to-all-start = ((s16[16,2,144,128]{3,2,1,0:T(8,128)(2,1)}), s16[16,2,144,128]{3,2,1,0:T(8,128)(2,1)S(1)}, u32[]{:S(2)}, u32[]{:S(2)}) async-start(s16[16,2,144,128]{3,2,1,0:T(8,128)(2,1)} %bitcast.11), calls=%async_computation | async-start | bytes 2359296 | tf_op jit(solution)/shard_map/all_to_all | solution.py:549
  11.6 0.0 collective-permute-done.mate_re
  11.6 0.0 copy-start
  11.6 0.0 collective-permute-done.1.mate_im
  11.6 1.3 %copy-done = f32[2,512,512]{2,1,0:T(8,128)} copy-done((f32[2,512,512]{2,1,0:T(8,128)}, f32[2,512,512]{2,1,0:T(8,128)S(1)}, u32[]{:S(2)}) %copy-start) | copy-done | bytes 2097176
  12.9 9.5 %round.1.tiles_ref = f32[2,4,2,2,512,128]{5,4,3,2,1,0:T(8,128)} custom-call(f32[2,512,512]{2,1,0:T(8,128)} %own_re.1, f32[2,512,512]{2,1,0:T(8,128)} %own_im.1, f32[2,512,512]{2,1,0:T(8,128)} %copy-done, f32[2,512,512]{2,1,0:T(8,128)} %collective-permute-done.1.mate_im), custom_call_target="tpu_custom_call" | custom-call | bytes 16777216 | tf_op jit(solution)/shard_map/round/pallas_call | solution.py:439
  22.5 6.4 %all-to-all-done = s16[16,2,144,128]{3,2,1,0:T(8,128)(2,1)S(1)} async-done(((s16[16,2,144,128]{3,2,1,0:T(8,128)(2,1)}), s16[16,2,144,128]{3,2,1,0:T(8,128)(2,1)S(1)}, u32[]{:S(2)}, u32[]{:S(2)}) %all-to-all-start) | async-done | bytes 1179680 | tf_op jit(solution)/shard_map/all_to_all | solution.py:549
  28.9 0.0 copy-start.1
  28.9 0.7 slice_convert_fusion
  29.6 0.4 copy-done.1
  30.0 21.8 %positions.1 = (bf16[32,4,128,128]{3,2,1,0:T(8,128)(2,1)}, f32[2,2,128,128]{3,2,1,0:T(8,128)}) custom-call(s32[32,2]{1,0:T(8,128)} %bitcast.16, s16[32,144,128]{2,1,0:T(8,128)(2,1)} %bitcast.13, f32[2,4,2,2,512,128]{5,4,3,2,1,0:T(8,128)} %round.1.tiles_ref, f32[2,2,128,128]{3,2,1,0:T(8,128)} %probe_in.1, bf16[8,256,256]{2,1,0:T(8,128)(2,1)} %constant.11.clone.tables_ref), custom_call_target="tpu_custom_call" | custom-call | flops 25769803776 | bytes 25165824 | tf_op jit(solution)/shard_map/positions/pallas_call | solution.py:455
  51.8 15.9 %all-to-all-start.1 = ((f32[128,4,128]{2,1,0:T(4,128)}), f32[128,4,128]{2,1,0:T(4,128)S(1)}, u32[]{:S(2)}, u32[]{:S(2)}) async-start(f32[128,4,128]{2,1,0:T(4,128)} %bitcast.15), calls=%async_computation.1 | async-start | bytes 524288 | tf_op jit(solution)/shard_map/all_to_all | solution.py:522
  67.8 7.2 %scatter.1 = (f32[2,2,512,512]{3,2,1,0:T(8,128)}, f32[2,2,512,512]{3,2,1,0:T(8,128)}) custom-call(s32[32,2]{1,0:T(8,128)} %bitcast.17, bf16[32,4,128,128]{3,2,1,0:T(8,128)(2,1)} %get-tuple-element.16.grad_in), custom_call_target="tpu_custom_call" | custom-call | bytes 20971520 | tf_op jit(solution)/shard_map/scatter/pallas_call | solution.py:494
  75.0 4.2 %all-to-all-done.1 = f32[128,4,128]{2,1,0:T(4,128)S(1)} async-done(((f32[128,4,128]{2,1,0:T(4,128)}), f32[128,4,128]{2,1,0:T(4,128)S(1)}, u32[]{:S(2)}, u32[]{:S(2)}) %all-to-all-start.1) | async-done | bytes 262176 | tf_op jit(solution)/shard_map/all_to_all | solution.py:522
  79.2 0.1 reduce_sum.9
  79.4 0.5 collective-permute-start.2
  79.8 0.7 broadcast_in_dim.9
  80.6 6.4 %all-to-all-start.2 = ((f32[128,4,128]{2,1,0:T(4,128)}), f32[128,4,128]{2,1,0:T(4,128)S(1)}, u32[]{:S(2)}, u32[]{:S(2)}) async-start(f32[128,4,128]{2,1,0:T(4,128)} %broadcast_in_dim.9), calls=%async_computation.2 | async-start | bytes 524288 | tf_op jit(solution)/shard_map/all_to_all | solution.py:526
  87.0 0.0 collective-permute-done.2
  87.1 6.5 %add.3 = f32[2,2,512,512]{3,2,1,0:T(8,128)} add(f32[2,2,512,512]{3,2,1,0:T(8,128)} %get-tuple-element.20, f32[2,2,512,512]{3,2,1,0:T(8,128)} %collective-permute-done.2) | non-fusion elementwise | flops 1048576 | bytes 12582912 | tf_op jit(solution)/shard_map/add | solution.py:527
  93.6 5.0 %all-to-all-done.2 = f32[128,4,128]{2,1,0:T(4,128)S(1)} async-done(((f32[128,4,128]{2,1,0:T(4,128)}), f32[128,4,128]{2,1,0:T(4,128)S(1)}, u32[]{:S(2)}, u32[]{:S(2)}) %all-to-all-start.2) | async-done | bytes 262176 | tf_op jit(solution)/shard_map/all_to_all | solution.py:526
  98.5 0.7 copy.17
  (1 shorter events, 0.0 us)
Async XLA Ops:
  0.6 11.0 %collective-permute-start = (f32[2,512,512]{2,1,0:T(8,128)}, f32[2,512,512]{2,1,0:T(8,128)S(1)}, u32[]{:S(2)}, u32[]{:S(2)}) collective-permute-start(f32[2,512,512]{2,1,0:T(8,128)} %own_re.1), channel_id=1, source_target_pairs={{0,1},{1,0},{2,3},{3,2},{4,5},{5,4},{6,7},{7,6},{8,9},{9,8},{10,11... | collective-permute-start | bytes 6291464 | tf_op jit(solution)/shard_map/ppermute | solution.py:552
  2.1 9.5 %collective-permute-start.1 = (f32[2,512,512]{2,1,0:T(8,128)}, f32[2,512,512]{2,1,0:T(8,128)}, u32[]{:S(2)}, u32[]{:S(2)}) collective-permute-start(f32[2,512,512]{2,1,0:T(8,128)} %own_im.1), channel_id=1, source_target_pairs={{0,1},{1,0},{2,3},{3,2},{4,5},{5,4},{6,7},{7,6},{8,9},{9,8},{10,11... | collective-permute-start | bytes 6291464 | tf_op jit(solution)/shard_map/ppermute | solution.py:553
  4.8 24.1 %all-to-all-start = ((s16[16,2,144,128]{3,2,1,0:T(8,128)(2,1)}), s16[16,2,144,128]{3,2,1,0:T(8,128)(2,1)S(1)}, u32[]{:S(2)}, u32[]{:S(2)}) async-start(s16[16,2,144,128]{3,2,1,0:T(8,128)(2,1)} %bitcast.11), calls=%async_computation | async-start | bytes 2359296 | tf_op jit(solution)/shard_map/all_to_all | solution.py:549
  11.6 1.3 %copy-start = (f32[2,512,512]{2,1,0:T(8,128)}, f32[2,512,512]{2,1,0:T(8,128)S(1)}, u32[]{:S(2)}) copy-start(f32[2,512,512]{2,1,0:T(8,128)S(1)} %collective-permute-done.mate_re) | copy-start | bytes 6291460
  28.9 1.1 %copy-start.1 = (s16[16,2,144,128]{3,2,1,0:T(8,128)(2,1)}, s16[16,2,144,128]{3,2,1,0:T(8,128)(2,1)S(1)}, u32[]{:S(2)}) copy-start(s16[16,2,144,128]{3,2,1,0:T(8,128)(2,1)S(1)} %all-to-all-done) | copy-start | bytes 3538948
  51.8 27.4 %all-to-all-start.1 = ((f32[128,4,128]{2,1,0:T(4,128)}), f32[128,4,128]{2,1,0:T(4,128)S(1)}, u32[]{:S(2)}, u32[]{:S(2)}) async-start(f32[128,4,128]{2,1,0:T(4,128)} %bitcast.15), calls=%async_computation.1 | async-start | bytes 524288 | tf_op jit(solution)/shard_map/all_to_all | solution.py:522
  79.4 7.7 %collective-permute-start.2 = (f32[2,2,512,512]{3,2,1,0:T(8,128)}, f32[2,2,512,512]{3,2,1,0:T(8,128)}, u32[]{:S(2)}, u32[]{:S(2)}) collective-permute-start(f32[2,2,512,512]{3,2,1,0:T(8,128)} %get-tuple-element.21), channel_id=1, source_target_pairs={{0,1},{1,0},{2,3},{3,2},{4,5},{5,4},{6,7},{7,6},{8,9},{9,8},{10,11... | collective-permute-start | bytes 12582920 | tf_op jit(solution)/shard_map/ppermute | solution.py:525
  80.6 17.9 %all-to-all-start.2 = ((f32[128,4,128]{2,1,0:T(4,128)}), f32[128,4,128]{2,1,0:T(4,128)S(1)}, u32[]{:S(2)}, u32[]{:S(2)}) async-start(f32[128,4,128]{2,1,0:T(4,128)} %broadcast_in_dim.9), calls=%async_computation.2 | async-start | bytes 524288 | tf_op jit(solution)/shard_map/all_to_all | solution.py:526

commit v5 on v4

--- a/solution.py
+++ b/solution.py
@@ -351,71 +351,54 @@
 
 
 def scatter_kernel(corner_ref, grad_in, own_out, mate_out, meta, grad, total, in_sem, out_sem):
-    n_mate, count = list_live(corner_ref, meta)
+    _, count = list_live(corner_ref, meta)
     n_groups = (count + UNROLL - 1) // UNROLL
-    mate_last = jnp.maximum((n_mate + UNROLL - 1) // UNROLL - 1, 0)
-
-    def grad_copy(group, half):
-        return pltpu.make_async_copy(
-            grad_in.at[pl.ds(group * UNROLL, UNROLL)], grad.at[half], in_sem.at[half]
-        )
-
-    def total_copies(tile):
-        out = (own_out, mate_out)[tile]
+
+    def grad_copy(group):
+        items = pl.ds(group * UNROLL, UNROLL)
+        return pltpu.make_async_copy(grad_in.at[items], grad.at[items], in_sem.at[group])
+
+    def fetch(group, carry):
+        grad_copy(group).start()
+        return carry
+
+    def total_copies(layer):
         return [
             pltpu.make_async_copy(
                 total.at[tile, pl.ds(2 * layer, 2), side],
                 out.at[layer, :, :, pl.ds(side * N, N)],
                 out_sem.at[tile, layer, side],
             )
-            for layer in range(2)
+            for tile, out in enumerate((own_out, mate_out))
             for side in range(TILE // N)
         ]
 
-    @pl.when(n_groups > 0)
-    def _():
-        grad_copy(0, 0).start()
-
+    lax.fori_loop(0, n_groups, fetch, 0)
     total[...] = jnp.zeros(total.shape, F32)
     lane = lax.broadcasted_iota(I32, (N, N), 1)
 
-    def step(group, carry):
-        half = lax.rem(group, 2)
-
-        @pl.when(group + 1 < n_groups)
-        def _():
-            grad_copy(group + 1, 1 - half).start()
-
-        grad_copy(group, half).wait()
-        for u in range(UNROLL):
-            item = group * UNROLL + u
-            row, col, tile = meta[1, item], meta[2, item], meta[3, item]
-            first = jnp.minimum(col // N, 2)
-            shift = col - first * N
-            for plane in range(4):
-                moved = pltpu.roll(grad[half, u, plane].astype(F32), lax.rem(shift, N), 1)
-                here = (tile, plane, first, pl.ds(row, N))
-                there = (tile, plane, first + 1, pl.ds(row, N))
-                total[here] = total[here] + jnp.where(lane >= shift, moved, 0.0)
-                total[there] = total[there] + jnp.where(lane < shift, moved, 0.0)
-
-        @pl.when(group == mate_last)
-        def _():
-            for copy in total_copies(1):
-                copy.start()
-
-        return carry
-
-    lax.fori_loop(0, n_groups, step, 0)
-
-    @pl.when(n_groups == 0)
-    def _():
-        for copy in total_copies(1):
+    for layer in (1, 0):
+
+        def step(group, carry, layer=layer):
+            if layer == 1:
+                grad_copy(group).wait()
+            for u in range(UNROLL):
+                item = group * UNROLL + u
+                row, col, tile = meta[1, item], meta[2, item], meta[3, item]
+                first = jnp.minimum(col // N, 2)
+                shift = col - first * N
+                for plane in (2 * layer, 2 * layer + 1):
+                    moved = pltpu.roll(grad[item, plane].astype(F32), lax.rem(shift, N), 1)
+                    here = (tile, plane, first, pl.ds(row, N))
+                    there = (tile, plane, first + 1, pl.ds(row, N))
+                    total[here] = total[here] + jnp.where(lane >= shift, moved, 0.0)
+                    total[there] = total[there] + jnp.where(lane < shift, moved, 0.0)
+            return carry
+
+        lax.fori_loop(0, n_groups, step, 0)
+        for copy in total_copies(layer):
             copy.start()
-
-    for copy in total_copies(0):
-        copy.start()
-    for copy in total_copies(0) + total_copies(1):
+    for copy in total_copies(1) + total_copies(0):
         copy.wait()
 
 
@@ -498,9 +481,9 @@
         out_specs=(ANY, ANY),
         scratch_shapes=[
             pltpu.SMEM((5, slots + UNROLL), I32),
-            pltpu.VMEM((2, UNROLL, 4, N, N), BF16),
+            pltpu.VMEM((slots, 4, N, N), BF16),
             pltpu.VMEM((2, 4, TILE // N, TILE, N), F32),
-            pltpu.SemaphoreType.DMA((2,)),
+            pltpu.SemaphoreType.DMA((slots // UNROLL,)),
             pltpu.SemaphoreType.DMA((2, 2, TILE // N)),
         ],
         compiler_params=PARAMS,

time: 101 us -> 98.8 us (0.978); the launches traced: 99.2 us -> 98.9 us
    all_to_all x1, starting transfers between devices: 6.45 us -> 4.93 us  [finish(): lax.all_to_all(jnp.broadcast_to(piece, parts.shape), axes, 0, 0, tiled=True)]
    ppermute x1, waiting for transfers between devices: 0.01 us -> 1.45 us  [finish(): other_grad = lax.ppermute(mate_grad, axes, mates)]
    all_to_all x1, waiting for transfers between devices: 4.96 us -> 3.52 us  [finish(): lax.all_to_all(jnp.broadcast_to(piece, parts.shape), axes, 0, 0, tiled=True)]
    all_to_all x1, starting transfers between devices: 15.9 us -> 17.1 us  [finish(): pieces = lax.all_to_all(parts, axes, 0, 0, tiled=True)]
  transfers between devices with their start and end apart: 6 -> 6, of which waited for: 3 -> 4; matrix products, arithmetic and copies ran while one was open for 7% -> 7% of each run, Pallas kernels for 19% -> 19%
where the time goes in v5:
time: 98.8 us; the launch traced here: 98.9 us
  Pallas kernels  40.5 us (41%)
  starting transfers between devices  30.9 us (31%)
  waiting for transfers between devices  16.3 us (16%)
  other arithmetic  7.31 us (7%)
  local copies, waits for them, and re-layouts  3.18 us (3%)
    pallas_call x1, Pallas kernels, run_positions(): pl.pallas_call(positions_kernel, out_shape=(jax.ShapeDtypeStruct((slots,...  21.9 us
    all_to_all x1, starting transfers between devices, finish(): pieces = lax.all_to_all(parts, axes, 0, 0, tiled=True)  17.1 us
    pallas_call x1, Pallas kernels, run_round(): pl.pallas_call(round_kernel, grid=(2, strips), out_shape=jax.ShapeDtypeSt...  9.52 us
    all_to_all x1, starting transfers between devices, body(): lax.all_to_all(requests.reshape(groups, CAP, N + TAIL, N), 'scan', 0, 0,...  6.84 us
    pallas_call x1, Pallas kernels, run_scatter(): pl.pallas_call(scatter_kernel, out_shape=(grad_shape, grad_shape), in_spe...  6.54 us
    add x1, other arithmetic, finish(): object_grad = own_grad + other_grad  6.49 us
    all_to_all x1, waiting for transfers between devices, body(): lax.all_to_all(requests.reshape(groups, CAP, N + TAIL, N), 'scan', 0, 0,...  6.44 us
    all_to_all x1, starting transfers between devices, finish(): lax.all_to_all(jnp.broadcast_to(piece, parts.shape), axes, 0, 0, tiled=True)  4.93 us
  transfers between devices with their start and end apart: 6, of which 4 were waited for; matrix products, arithmetic and copies ran while one was open for 7% of the time, Pallas kernels for 19%

profile of v5, /device:TPU:1, one launch (start us, length us, event | category | flops | bytes accessed | tf_op | source)
XLA Modules:
  0.0 98.9 jit_solution(11547851920098461560)
XLA Ops:
  0.6 1.5 %collective-permute-start = (f32[2,512,512]{2,1,0:T(8,128)}, f32[2,512,512]{2,1,0:T(8,128)S(1)}, u32[]{:S(2)}, u32[]{:S(2)}) collective-permute-start(f32[2,512,512]{2,1,0:T(8,128)} %own_re.1), channel_id=1, source_target_pairs={{0,1},{1,0},{2,3},{3,2},{4,5},{5,4},{6,7},{7,6},{8,9},{9,8},{10,11... | collective-permute-start | bytes 6291464 | tf_op jit(solution)/shard_map/ppermute | solution.py:535
  2.1 0.1 collective-permute-start.1
  2.2 2.5 %prepare.1 = s16[32,144,128]{2,1,0:T(8,128)(2,1)} custom-call(s32[1]{0:T(128)} %bitcast.me_ref, s32[16]{0:T(128)} %bitcast.20, s32[2,16]{1,0:T(2,128)} %bitcast.19, f32[16,128,128]{2,1,0:T(8,128)} %amplitudes_ref.1), custom_call_target="tpu_custom_call" | custom-call | tf_op jit(solution)/shard_map/prepare/pallas_call | solution.py:523
  4.8 6.8 %all-to-all-start = ((s16[16,2,144,128]{3,2,1,0:T(8,128)(2,1)}), s16[16,2,144,128]{3,2,1,0:T(8,128)(2,1)S(1)}, u32[]{:S(2)}, u32[]{:S(2)}) async-start(s16[16,2,144,128]{3,2,1,0:T(8,128)(2,1)} %bitcast.11), calls=%async_computation | async-start | bytes 2359296 | tf_op jit(solution)/shard_map/all_to_all | solution.py:532
  11.6 0.0 collective-permute-done.mate_re
  11.6 0.0 copy-start
  11.6 0.0 collective-permute-done.1.mate_im
  11.6 1.3 %copy-done = f32[2,512,512]{2,1,0:T(8,128)} copy-done((f32[2,512,512]{2,1,0:T(8,128)}, f32[2,512,512]{2,1,0:T(8,128)S(1)}, u32[]{:S(2)}) %copy-start) | copy-done | bytes 2097176
  12.9 9.5 %round.1.tiles_ref = f32[2,4,2,2,512,128]{5,4,3,2,1,0:T(8,128)} custom-call(f32[2,512,512]{2,1,0:T(8,128)} %own_re.1, f32[2,512,512]{2,1,0:T(8,128)} %own_im.1, f32[2,512,512]{2,1,0:T(8,128)} %copy-done, f32[2,512,512]{2,1,0:T(8,128)} %collective-permute-done.1.mate_im), custom_call_target="tpu_custom_call" | custom-call | bytes 16777216 | tf_op jit(solution)/shard_map/round/pallas_call | solution.py:422
  22.5 6.4 %all-to-all-done = s16[16,2,144,128]{3,2,1,0:T(8,128)(2,1)S(1)} async-done(((s16[16,2,144,128]{3,2,1,0:T(8,128)(2,1)}), s16[16,2,144,128]{3,2,1,0:T(8,128)(2,1)S(1)}, u32[]{:S(2)}, u32[]{:S(2)}) %all-to-all-start) | async-done | bytes 1179680 | tf_op jit(solution)/shard_map/all_to_all | solution.py:532
  28.9 0.0 copy-start.1
  28.9 0.7 slice_convert_fusion
  29.6 0.4 copy-done.1
  30.0 21.9 %positions.1 = (bf16[32,4,128,128]{3,2,1,0:T(8,128)(2,1)}, f32[2,2,128,128]{3,2,1,0:T(8,128)}) custom-call(s32[32,2]{1,0:T(8,128)} %bitcast.16, s16[32,144,128]{2,1,0:T(8,128)(2,1)} %bitcast.13, f32[2,4,2,2,512,128]{5,4,3,2,1,0:T(8,128)} %round.1.tiles_ref, f32[2,2,128,128]{3,2,1,0:T(8,128)} %probe_in.1, bf16[8,256,256]{2,1,0:T(8,128)(2,1)} %constant.11.clone.tables_ref), custom_call_target="tpu_custom_call" | custom-call | flops 25769803776 | bytes 25165824 | tf_op jit(solution)/shard_map/positions/pallas_call | solution.py:438
  51.9 17.1 %all-to-all-start.1 = ((f32[128,4,128]{2,1,0:T(4,128)}), f32[128,4,128]{2,1,0:T(4,128)S(1)}, u32[]{:S(2)}, u32[]{:S(2)}) async-start(f32[128,4,128]{2,1,0:T(4,128)} %bitcast.15), calls=%async_computation.1 | async-start | bytes 524288 | tf_op jit(solution)/shard_map/all_to_all | solution.py:505
  68.9 6.5 %scatter.1 = (f32[2,2,512,512]{3,2,1,0:T(8,128)}, f32[2,2,512,512]{3,2,1,0:T(8,128)}) custom-call(s32[32,2]{1,0:T(8,128)} %bitcast.17, bf16[32,4,128,128]{3,2,1,0:T(8,128)(2,1)} %get-tuple-element.16.grad_in), custom_call_target="tpu_custom_call" | custom-call | bytes 20971520 | tf_op jit(solution)/shard_map/scatter/pallas_call | solution.py:477
  75.5 4.9 %all-to-all-done.1 = f32[128,4,128]{2,1,0:T(4,128)S(1)} async-done(((f32[128,4,128]{2,1,0:T(4,128)}), f32[128,4,128]{2,1,0:T(4,128)S(1)}, u32[]{:S(2)}, u32[]{:S(2)}) %all-to-all-start.1) | async-done | bytes 262176 | tf_op jit(solution)/shard_map/all_to_all | solution.py:505
  80.4 0.1 reduce_sum.9
  80.6 0.5 collective-permute-start.2
  81.0 0.7 broadcast_in_dim.9
  81.8 4.9 %all-to-all-start.2 = ((f32[128,4,128]{2,1,0:T(4,128)}), f32[128,4,128]{2,1,0:T(4,128)S(1)}, u32[]{:S(2)}, u32[]{:S(2)}) async-start(f32[128,4,128]{2,1,0:T(4,128)} %broadcast_in_dim.9), calls=%async_computation.2 | async-start | bytes 524288 | tf_op jit(solution)/shard_map/all_to_all | solution.py:509
  86.7 1.5 %collective-permute-done.2 = f32[2,2,512,512]{3,2,1,0:T(8,128)} collective-permute-done((f32[2,2,512,512]{3,2,1,0:T(8,128)}, f32[2,2,512,512]{3,2,1,0:T(8,128)}, u32[]{:S(2)}, u32[]{:S(2)}) %collective-permute-start.2) | collective-permute-done | bytes 4194336 | tf_op jit(solution)/shard_map/ppermute | solution.py:508
  88.2 6.5 %add.3 = f32[2,2,512,512]{3,2,1,0:T(8,128)} add(f32[2,2,512,512]{3,2,1,0:T(8,128)} %get-tuple-element.20, f32[2,2,512,512]{3,2,1,0:T(8,128)} %collective-permute-done.2) | non-fusion elementwise | flops 1048576 | bytes 12582912 | tf_op jit(solution)/shard_map/add | solution.py:510
  94.6 3.5 %all-to-all-done.2 = f32[128,4,128]{2,1,0:T(4,128)S(1)} async-done(((f32[128,4,128]{2,1,0:T(4,128)}), f32[128,4,128]{2,1,0:T(4,128)S(1)}, u32[]{:S(2)}, u32[]{:S(2)}) %all-to-all-start.2) | async-done | bytes 262176 | tf_op jit(solution)/shard_map/all_to_all | solution.py:509
  98.2 0.7 copy.17
  (1 shorter events, 0.0 us)
Async XLA Ops:
  0.6 11.0 %collective-permute-start = (f32[2,512,512]{2,1,0:T(8,128)}, f32[2,512,512]{2,1,0:T(8,128)S(1)}, u32[]{:S(2)}, u32[]{:S(2)}) collective-permute-start(f32[2,512,512]{2,1,0:T(8,128)} %own_re.1), channel_id=1, source_target_pairs={{0,1},{1,0},{2,3},{3,2},{4,5},{5,4},{6,7},{7,6},{8,9},{9,8},{10,11... | collective-permute-start | bytes 6291464 | tf_op jit(solution)/shard_map/ppermute | solution.py:535
  2.1 9.5 %collective-permute-start.1 = (f32[2,512,512]{2,1,0:T(8,128)}, f32[2,512,512]{2,1,0:T(8,128)}, u32[]{:S(2)}, u32[]{:S(2)}) collective-permute-start(f32[2,512,512]{2,1,0:T(8,128)} %own_im.1), channel_id=1, source_target_pairs={{0,1},{1,0},{2,3},{3,2},{4,5},{5,4},{6,7},{7,6},{8,9},{9,8},{10,11... | collective-permute-start | bytes 6291464 | tf_op jit(solution)/shard_map/ppermute | solution.py:536
  4.8 24.1 %all-to-all-start = ((s16[16,2,144,128]{3,2,1,0:T(8,128)(2,1)}), s16[16,2,144,128]{3,2,1,0:T(8,128)(2,1)S(1)}, u32[]{:S(2)}, u32[]{:S(2)}) async-start(s16[16,2,144,128]{3,2,1,0:T(8,128)(2,1)} %bitcast.11), calls=%async_computation | async-start | bytes 2359296 | tf_op jit(solution)/shard_map/all_to_all | solution.py:532
  11.6 1.3 %copy-start = (f32[2,512,512]{2,1,0:T(8,128)}, f32[2,512,512]{2,1,0:T(8,128)S(1)}, u32[]{:S(2)}) copy-start(f32[2,512,512]{2,1,0:T(8,128)S(1)} %collective-permute-done.mate_re) | copy-start | bytes 6291460
  28.9 1.1 %copy-start.1 = (s16[16,2,144,128]{3,2,1,0:T(8,128)(2,1)}, s16[16,2,144,128]{3,2,1,0:T(8,128)(2,1)S(1)}, u32[]{:S(2)}) copy-start(s16[16,2,144,128]{3,2,1,0:T(8,128)(2,1)S(1)} %all-to-all-done) | copy-start | bytes 3538948
  51.9 28.5 %all-to-all-start.1 = ((f32[128,4,128]{2,1,0:T(4,128)}), f32[128,4,128]{2,1,0:T(4,128)S(1)}, u32[]{:S(2)}, u32[]{:S(2)}) async-start(f32[128,4,128]{2,1,0:T(4,128)} %bitcast.15), calls=%async_computation.1 | async-start | bytes 524288 | tf_op jit(solution)/shard_map/all_to_all | solution.py:505
  80.6 7.6 %collective-permute-start.2 = (f32[2,2,512,512]{3,2,1,0:T(8,128)}, f32[2,2,512,512]{3,2,1,0:T(8,128)}, u32[]{:S(2)}, u32[]{:S(2)}) collective-permute-start(f32[2,2,512,512]{3,2,1,0:T(8,128)} %get-tuple-element.21), channel_id=1, source_target_pairs={{0,1},{1,0},{2,3},{3,2},{4,5},{5,4},{6,7},{7,6},{8,9},{9,8},{10,11... | collective-permute-start | bytes 12582920 | tf_op jit(solution)/shard_map/ppermute | solution.py:508
  81.8 16.4 %all-to-all-start.2 = ((f32[128,4,128]{2,1,0:T(4,128)}), f32[128,4,128]{2,1,0:T(4,128)S(1)}, u32[]{:S(2)}, u32[]{:S(2)}) async-start(f32[128,4,128]{2,1,0:T(4,128)} %broadcast_in_dim.9), calls=%async_computation.2 | async-start | bytes 524288 | tf_op jit(solution)/shard_map/all_to_all | solution.py:509

commit v6 on v5

--- a/solution.py
+++ b/solution.py
@@ -172,14 +172,47 @@
     table_copy.wait()
     probe_copy.wait()
 
+    def enter(group, buffer):
+        row, col = meta[1, group * UNROLL], meta[2, group * UNROLL]
+        shift = col - jnp.minimum(col // N, 2) * N
+        row_in = row - jnp.minimum(row // 8 * 8, TILE - WIN_ROWS)
+
+        def cut(part):
+            def piece():
+                move = lax.rem(N - shift, N)
+                near = window[buffer, 0, 0, part, 0, pl.ds(row_in, N), :]
+                far = window[buffer, 0, 1, part, 0, pl.ds(row_in, N), :]
+                patch[0, part] = jnp.where(
+                    lane < N - shift, pltpu.roll(near, move, 1), pltpu.roll(far, move, 1)
+                )
+
+            return piece
+
+        def times(m, c):
+            def piece():
+                p_re, p_im = patch[0, 0], patch[0, 1]
+                w_re, w_im = probe_ref[m, 0], probe_ref[m, 1]
+                value = w_re * p_re - w_im * p_im if c == 0 else w_im * p_re + w_re * p_im
+                big, small = split(value)
+                high[0, halves[m], halves[c]] = big
+                low[0, halves[m], halves[c]] = small
+
+            return piece
+
+        return [cut(0), cut(1)] + [times(m, c) for m in range(2) for c in range(2)]
+
+    @pl.when(n_groups > 0)
+    def _():
+        window_copies(0, 0, False)
+        for piece in enter(0, 0):
+            piece()
+
     def step(group, carry):
         buffer = lax.rem(group, 2)
 
         @pl.when(group + 1 < n_groups)
         def _():
             window_copies(group + 1, 1 - buffer, True)
-
-        window_copies(group, buffer, False)
 
         @pl.when(group >= 2)
         def _():
@@ -312,8 +345,6 @@
             ("left", 0, field, lambda u: swap_blocks(u, field), exit_gradient),
         )
         jobs = [(s, u) for s in range(len(stages)) for u in range(UNROLL)]
-        for piece in stages[0][3](0):
-            piece()
         for at, (s, u) in enumerate(jobs):
             side, form, result, _, beside = stages[s]
             pieces = list(beside(u))
@@ -322,6 +353,13 @@
                 pieces = list(stages[s_next][3](u_next)) + pieces
             if s == len(stages) - 1 and u > 0:
                 pieces += entry_gradient(u - 1)
+            if at + 1 == len(jobs):
+
+                @pl.when(group + 1 < n_groups)
+                def _():
+                    window_copies(group + 1, 1 - buffer, False)
+
+                pieces += enter(group + 1, 1 - buffer)
             cuts = [(len(pieces) * k + 2) // 3 for k in range(4)]
             big, small = high[u], low[u]
             sums = None

time: 98.8 us -> 97.1 us (0.983)
  starting transfers between devices: 30.9 us -> 29.1 us
    all_to_all x1, starting transfers between devices: 17.1 us -> 15.2 us  [finish(): pieces = lax.all_to_all(parts, axes, 0, 0, tiled=True)]
where the time goes in v6:
time: 97.1 us; the launch traced here: 96.5 us
  Pallas kernels  39.9 us (41%)
  starting transfers between devices  29.1 us (30%)
  waiting for transfers between devices  16.3 us (17%)
  other arithmetic  7.31 us (8%)
  local copies, waits for them, and re-layouts  3.18 us (3%)
    pallas_call x1, Pallas kernels, run_positions(): pl.pallas_call(positions_kernel, out_shape=(jax.ShapeDtypeStruct((slots,...  21.3 us
    all_to_all x1, starting transfers between devices, finish(): pieces = lax.all_to_all(parts, axes, 0, 0, tiled=True)  15.2 us
    pallas_call x1, Pallas kernels, run_round(): pl.pallas_call(round_kernel, grid=(2, strips), out_shape=jax.ShapeDtypeSt...  9.52 us
    all_to_all x1, starting transfers between devices, body(): lax.all_to_all(requests.reshape(groups, CAP, N + TAIL, N), 'scan', 0, 0,...  6.84 us
    pallas_call x1, Pallas kernels, run_scatter(): pl.pallas_call(scatter_kernel, out_shape=(grad_shape, grad_shape), in_spe...  6.54 us
    add x1, other arithmetic, finish(): object_grad = own_grad + other_grad  6.49 us
    all_to_all x1, waiting for transfers between devices, body(): lax.all_to_all(requests.reshape(groups, CAP, N + TAIL, N), 'scan', 0, 0,...  6.44 us
    all_to_all x1, starting transfers between devices, finish(): lax.all_to_all(jnp.broadcast_to(piece, parts.shape), axes, 0, 0, tiled=True)  4.95 us
  transfers between devices with their start and end apart: 6, of which 4 were waited for; matrix products, arithmetic and copies ran while one was open for 7% of the time, Pallas kernels for 19%

profile of v6, /device:TPU:1, one launch (start us, length us, event | category | flops | bytes accessed | tf_op | source)
XLA Modules:
  0.0 96.5 jit_solution(15059289055252786528)
XLA Ops:
  0.6 1.5 %collective-permute-start = (f32[2,512,512]{2,1,0:T(8,128)}, f32[2,512,512]{2,1,0:T(8,128)S(1)}, u32[]{:S(2)}, u32[]{:S(2)}) collective-permute-start(f32[2,512,512]{2,1,0:T(8,128)} %own_re.1), channel_id=1, source_target_pairs={{0,1},{1,0},{2,3},{3,2},{4,5},{5,4},{6,7},{7,6},{8,9},{9,8},{10,11... | collective-permute-start | bytes 6291464 | tf_op jit(solution)/shard_map/ppermute | solution.py:573
  2.1 0.1 collective-permute-start.1
  2.2 2.5 %prepare.1 = s16[32,144,128]{2,1,0:T(8,128)(2,1)} custom-call(s32[1]{0:T(128)} %bitcast.me_ref, s32[16]{0:T(128)} %bitcast.20, s32[2,16]{1,0:T(2,128)} %bitcast.19, f32[16,128,128]{2,1,0:T(8,128)} %amplitudes_ref.1), custom_call_target="tpu_custom_call" | custom-call | tf_op jit(solution)/shard_map/prepare/pallas_call | solution.py:561
  4.8 6.8 %all-to-all-start = ((s16[16,2,144,128]{3,2,1,0:T(8,128)(2,1)}), s16[16,2,144,128]{3,2,1,0:T(8,128)(2,1)S(1)}, u32[]{:S(2)}, u32[]{:S(2)}) async-start(s16[16,2,144,128]{3,2,1,0:T(8,128)(2,1)} %bitcast.11), calls=%async_computation | async-start | bytes 2359296 | tf_op jit(solution)/shard_map/all_to_all | solution.py:570
  11.6 0.0 collective-permute-done.mate_re
  11.6 0.0 copy-start
  11.6 0.0 collective-permute-done.1.mate_im
  11.6 1.3 %copy-done = f32[2,512,512]{2,1,0:T(8,128)} copy-done((f32[2,512,512]{2,1,0:T(8,128)}, f32[2,512,512]{2,1,0:T(8,128)S(1)}, u32[]{:S(2)}) %copy-start) | copy-done | bytes 2097176
  12.9 9.5 %round.1.tiles_ref = f32[2,4,2,2,512,128]{5,4,3,2,1,0:T(8,128)} custom-call(f32[2,512,512]{2,1,0:T(8,128)} %own_re.1, f32[2,512,512]{2,1,0:T(8,128)} %own_im.1, f32[2,512,512]{2,1,0:T(8,128)} %copy-done, f32[2,512,512]{2,1,0:T(8,128)} %collective-permute-done.1.mate_im), custom_call_target="tpu_custom_call" | custom-call | bytes 16777216 | tf_op jit(solution)/shard_map/round/pallas_call | solution.py:460
  22.5 6.4 %all-to-all-done = s16[16,2,144,128]{3,2,1,0:T(8,128)(2,1)S(1)} async-done(((s16[16,2,144,128]{3,2,1,0:T(8,128)(2,1)}), s16[16,2,144,128]{3,2,1,0:T(8,128)(2,1)S(1)}, u32[]{:S(2)}, u32[]{:S(2)}) %all-to-all-start) | async-done | bytes 1179680 | tf_op jit(solution)/shard_map/all_to_all | solution.py:570
  28.9 0.0 copy-start.1
  28.9 0.7 slice_convert_fusion
  29.6 0.4 copy-done.1
  30.0 21.3 %positions.1 = (bf16[32,4,128,128]{3,2,1,0:T(8,128)(2,1)}, f32[2,2,128,128]{3,2,1,0:T(8,128)}) custom-call(s32[32,2]{1,0:T(8,128)} %bitcast.16, s16[32,144,128]{2,1,0:T(8,128)(2,1)} %bitcast.13, f32[2,4,2,2,512,128]{5,4,3,2,1,0:T(8,128)} %round.1.tiles_ref, f32[2,2,128,128]{3,2,1,0:T(8,128)} %probe_in.1, bf16[8,256,256]{2,1,0:T(8,128)(2,1)} %constant.11.clone.tables_ref), custom_call_target="tpu_custom_call" | custom-call | flops 25769803776 | bytes 25165824 | tf_op jit(solution)/shard_map/positions/pallas_call | solution.py:476
  51.3 15.2 %all-to-all-start.1 = ((f32[128,4,128]{2,1,0:T(4,128)}), f32[128,4,128]{2,1,0:T(4,128)S(1)}, u32[]{:S(2)}, u32[]{:S(2)}) async-start(f32[128,4,128]{2,1,0:T(4,128)} %bitcast.15), calls=%async_computation.1 | async-start | bytes 524288 | tf_op jit(solution)/shard_map/all_to_all | solution.py:543
  66.5 6.5 %scatter.1 = (f32[2,2,512,512]{3,2,1,0:T(8,128)}, f32[2,2,512,512]{3,2,1,0:T(8,128)}) custom-call(s32[32,2]{1,0:T(8,128)} %bitcast.17, bf16[32,4,128,128]{3,2,1,0:T(8,128)(2,1)} %get-tuple-element.16.grad_in), custom_call_target="tpu_custom_call" | custom-call | bytes 20971520 | tf_op jit(solution)/shard_map/scatter/pallas_call | solution.py:515
  73.1 4.9 %all-to-all-done.1 = f32[128,4,128]{2,1,0:T(4,128)S(1)} async-done(((f32[128,4,128]{2,1,0:T(4,128)}), f32[128,4,128]{2,1,0:T(4,128)S(1)}, u32[]{:S(2)}, u32[]{:S(2)}) %all-to-all-start.1) | async-done | bytes 262176 | tf_op jit(solution)/shard_map/all_to_all | solution.py:543
  78.0 0.1 reduce_sum.9
  78.1 0.5 collective-permute-start.2
  78.6 0.7 broadcast_in_dim.9
  79.3 5.0 %all-to-all-start.2 = ((f32[128,4,128]{2,1,0:T(4,128)}), f32[128,4,128]{2,1,0:T(4,128)S(1)}, u32[]{:S(2)}, u32[]{:S(2)}) async-start(f32[128,4,128]{2,1,0:T(4,128)} %broadcast_in_dim.9), calls=%async_computation.2 | async-start | bytes 524288 | tf_op jit(solution)/shard_map/all_to_all | solution.py:547
  84.3 1.4 %collective-permute-done.2 = f32[2,2,512,512]{3,2,1,0:T(8,128)} collective-permute-done((f32[2,2,512,512]{3,2,1,0:T(8,128)}, f32[2,2,512,512]{3,2,1,0:T(8,128)}, u32[]{:S(2)}, u32[]{:S(2)}) %collective-permute-start.2) | collective-permute-done | bytes 4194336 | tf_op jit(solution)/shard_map/ppermute | solution.py:546
  85.7 6.5 %add.3 = f32[2,2,512,512]{3,2,1,0:T(8,128)} add(f32[2,2,512,512]{3,2,1,0:T(8,128)} %get-tuple-element.20, f32[2,2,512,512]{3,2,1,0:T(8,128)} %collective-permute-done.2) | non-fusion elementwise | flops 1048576 | bytes 12582912 | tf_op jit(solution)/shard_map/add | solution.py:548
  92.2 3.5 %all-to-all-done.2 = f32[128,4,128]{2,1,0:T(4,128)S(1)} async-done(((f32[128,4,128]{2,1,0:T(4,128)}), f32[128,4,128]{2,1,0:T(4,128)S(1)}, u32[]{:S(2)}, u32[]{:S(2)}) %all-to-all-start.2) | async-done | bytes 262176 | tf_op jit(solution)/shard_map/all_to_all | solution.py:547
  95.8 0.7 copy.17
  (1 shorter events, 0.0 us)
Async XLA Ops:
  0.6 11.0 %collective-permute-start = (f32[2,512,512]{2,1,0:T(8,128)}, f32[2,512,512]{2,1,0:T(8,128)S(1)}, u32[]{:S(2)}, u32[]{:S(2)}) collective-permute-start(f32[2,512,512]{2,1,0:T(8,128)} %own_re.1), channel_id=1, source_target_pairs={{0,1},{1,0},{2,3},{3,2},{4,5},{5,4},{6,7},{7,6},{8,9},{9,8},{10,11... | collective-permute-start | bytes 6291464 | tf_op jit(solution)/shard_map/ppermute | solution.py:573
  2.1 9.5 %collective-permute-start.1 = (f32[2,512,512]{2,1,0:T(8,128)}, f32[2,512,512]{2,1,0:T(8,128)}, u32[]{:S(2)}, u32[]{:S(2)}) collective-permute-start(f32[2,512,512]{2,1,0:T(8,128)} %own_im.1), channel_id=1, source_target_pairs={{0,1},{1,0},{2,3},{3,2},{4,5},{5,4},{6,7},{7,6},{8,9},{9,8},{10,11... | collective-permute-start | bytes 6291464 | tf_op jit(solution)/shard_map/ppermute | solution.py:574
  4.8 24.1 %all-to-all-start = ((s16[16,2,144,128]{3,2,1,0:T(8,128)(2,1)}), s16[16,2,144,128]{3,2,1,0:T(8,128)(2,1)S(1)}, u32[]{:S(2)}, u32[]{:S(2)}) async-start(s16[16,2,144,128]{3,2,1,0:T(8,128)(2,1)} %bitcast.11), calls=%async_computation | async-start | bytes 2359296 | tf_op jit(solution)/shard_map/all_to_all | solution.py:570
  11.6 1.3 %copy-start = (f32[2,512,512]{2,1,0:T(8,128)}, f32[2,512,512]{2,1,0:T(8,128)S(1)}, u32[]{:S(2)}) copy-start(f32[2,512,512]{2,1,0:T(8,128)S(1)} %collective-permute-done.mate_re) | copy-start | bytes 6291460
  28.9 1.1 %copy-start.1 = (s16[16,2,144,128]{3,2,1,0:T(8,128)(2,1)}, s16[16,2,144,128]{3,2,1,0:T(8,128)(2,1)S(1)}, u32[]{:S(2)}) copy-start(s16[16,2,144,128]{3,2,1,0:T(8,128)(2,1)S(1)} %all-to-all-done) | copy-start | bytes 3538948
  51.3 26.7 %all-to-all-start.1 = ((f32[128,4,128]{2,1,0:T(4,128)}), f32[128,4,128]{2,1,0:T(4,128)S(1)}, u32[]{:S(2)}, u32[]{:S(2)}) async-start(f32[128,4,128]{2,1,0:T(4,128)} %bitcast.15), calls=%async_computation.1 | async-start | bytes 524288 | tf_op jit(solution)/shard_map/all_to_all | solution.py:543
  78.1 7.6 %collective-permute-start.2 = (f32[2,2,512,512]{3,2,1,0:T(8,128)}, f32[2,2,512,512]{3,2,1,0:T(8,128)}, u32[]{:S(2)}, u32[]{:S(2)}) collective-permute-start(f32[2,2,512,512]{3,2,1,0:T(8,128)} %get-tuple-element.21), channel_id=1, source_target_pairs={{0,1},{1,0},{2,3},{3,2},{4,5},{5,4},{6,7},{7,6},{8,9},{9,8},{10,11... | collective-permute-start | bytes 12582920 | tf_op jit(solution)/shard_map/ppermute | solution.py:546
  79.3 16.4 %all-to-all-start.2 = ((f32[128,4,128]{2,1,0:T(4,128)}), f32[128,4,128]{2,1,0:T(4,128)S(1)}, u32[]{:S(2)}, u32[]{:S(2)}) async-start(f32[128,4,128]{2,1,0:T(4,128)} %broadcast_in_dim.9), calls=%async_computation.2 | async-start | bytes 524288 | tf_op jit(solution)/shard_map/all_to_all | solution.py:547
